TPU v7x, 32 devices: a whole 2x2x4 slice. The times are simulated.
32 devices in a mesh: dp: 8 (over y, x, core), tensor: 4 (over z).
Axes of the slice: x: 2, y: 2, z: 4, core: 2. Of those that a mesh axis runs over, the one named last changes fastest.
Arguments:
- tokens: bfloat16 [32768, 512], P(('dp', 'tensor')), may hold values from -6 to 6
- cotangent: bfloat16 [32768, 512], P(('dp', 'tensor')), may hold values from -6 to 6
- seq_lengths: int32 [8, 2], P('dp'), may hold values from 1023 to 3073, as said below
- features: bfloat16 [8, 64, 256], replicated, may hold values from -6 to 6
- ln1_gain: float32 [512], replicated, may hold values from 0.1 to 1.9
- w_qkv: bfloat16 [512, 1536], replicated, may hold values from -0.25 to 0.25
- w_out: bfloat16 [512, 512], replicated, may hold values from -1.5 to 1.5
- b_out: bfloat16 [512], replicated, may hold values from -2 to 2
- ln2_gain: float32 [512], replicated, may hold values from 0.1 to 1.9
- w_in: bfloat16 [512, 2048], P(None, 'tensor'), may hold values from -0.25 to 0.25
- b_in: bfloat16 [2048], P('tensor'), may hold values from -2 to 2
- w_down: bfloat16 [2048, 512], P('tensor'), may hold values from -0.125 to 0.125
- b_down: bfloat16 [512], replicated, may hold values from -2 to 2
Outputs:
- layer_out: bfloat16 [32768, 512], P(('dp', 'tensor'))
- input_grad: float32 [32768, 512], P(('dp', 'tensor'))
- grad_ln1_gain: float32 [512], replicated
- grad_w_qkv: float32 [512, 1536], replicated
- grad_w_out: float32 [512, 512], replicated
- grad_b_out: float32 [512], replicated
- grad_ln2_gain: float32 [512], replicated
- grad_w_in: float32 [512, 2048], P(None, 'tensor')
- grad_b_in: float32 [2048], P('tensor')
- grad_w_down: float32 [2048, 512], P('tensor')
- grad_b_down: float32 [512], replicated
Inputs may be any that keep to these rules, and one draw needn't show every extreme that they name: `seq_lengths`: each row sums to 4096: one sequence of exactly 3073 rows and one of 1023 rows, in a drawn order.
All inputs are finite; a program needn't handle non-finite values.
Results may differ from a plain program's by a relative error of at most 0.019.
The roundings to bfloat16 on the way count: a program that leaves them out, or rounds other values in their place, can miss the bound.
Values may be sent and summed in bfloat16 or wider, within the bound.
A program may use at most 192 MiB of HBM per device.

v0:
```python
import jax
import jax.numpy as jnp
from jax import lax
from jax.sharding import PartitionSpec as P

EPSILON = 1e-05


def prefix(value, axis, combine, identity, reverse):
    size, index = (lax.axis_size(axis), lax.axis_index(axis))
    everything = jax.tree.map(lambda part: lax.all_gather(part, axis), value)
    start = jax.tree.map(
        lambda part, zero: jnp.broadcast_to(jnp.asarray(zero, part.dtype), part.shape),
        value,
        identity,
    )

    def turn(k, before):
        at = size - 1 - k if reverse else k
        reached = at > index if reverse else at < index
        new = combine(before, jax.tree.map(lambda part: part[at], everything))
        return jax.tree.map(lambda a, b: jnp.where(reached, a, b), new, before)

    return lax.fori_loop(0, size, turn, start)


def normalize(values):
    centre = jnp.mean(values, -1, keepdims=True)
    shifted = values - centre
    inverse = lax.rsqrt(jnp.mean(shifted * shifted, -1, keepdims=True) + EPSILON)
    return (shifted * inverse, inverse)


def normalize_back(upstream, gain, scaled, inverse):
    weighted = upstream * gain
    inner_mean = jnp.mean(weighted, -1, keepdims=True)
    cross_mean = jnp.mean(weighted * scaled, -1, keepdims=True)
    return (inverse * (weighted - inner_mean - scaled * cross_mean), jnp.sum(upstream * scaled, 0))


def feature_map(values, feature_table, width):
    project = jnp.einsum("rhd,hdm->rhm", values, feature_table, preferred_element_type=jnp.float32)
    widened = values.astype(jnp.float32)
    argument = project - 0.5 * jnp.sum(widened * widened, -1, keepdims=True)
    exact = jnp.exp(argument) * width ** (-0.5)
    return (exact, exact.astype(jnp.bfloat16))


def link_states(earlier, later):
    passing = 1.0 - later[2]
    return (
        later[0] + passing * earlier[0],
        later[1] + passing * earlier[1],
        jnp.maximum(earlier[2], later[2]),
    )


def pair_mask(segment):
    row_index = jnp.arange(segment.shape[0])
    return (row_index[:, None] >= row_index[None, :]) & (segment[:, None] == segment[None, :])


def gelu_back(inner_pre, act_grad):
    _, pullback = jax.vjp(jax.nn.gelu, inner_pre)
    return pullback(act_grad)[0].astype(jnp.bfloat16)


def forward_block(carried, inputs):
    states, totals, previous = carried
    query_feat, key_feat, values, segment = inputs
    scores = jnp.einsum("ihm,jhm->hij", query_feat, key_feat, preferred_element_type=jnp.float32)
    masked = jnp.where(pair_mask(segment)[None], scores, 0.0)
    reached = (segment == previous).astype(jnp.float32)[:, None]
    numerator = jnp.einsum(
        "hij,jhe->ihe", masked.astype(jnp.bfloat16), values, preferred_element_type=jnp.float32
    )
    outer_num = jnp.einsum(
        "ihm,hme->ihe", query_feat, states.astype(jnp.bfloat16), preferred_element_type=jnp.float32
    )
    numerator = numerator + reached[:, :, None] * outer_num
    outer_den = jnp.einsum(
        "ihm,hm->ih", query_feat, totals.astype(jnp.bfloat16), preferred_element_type=jnp.float32
    )
    denominator = jnp.sum(masked, -1).T + reached * outer_den
    closing = segment[-1]
    ending = (segment == closing)[:, None, None]
    keeping = previous == closing
    picked = jnp.where(ending, key_feat, jnp.zeros_like(key_feat))
    increment = jnp.einsum("jhm,jhe->hme", picked, values, preferred_element_type=jnp.float32)
    new_states = jnp.where(keeping, states, 0.0) + increment
    new_totals = jnp.where(keeping, totals, 0.0) + jnp.sum(picked.astype(jnp.float32), 0)
    return ((new_states, new_totals, closing), (numerator, denominator, states, totals, previous))


def backward_block(carried, inputs):
    grad_states, grad_totals = carried
    query_feat, key_feat, values, segment, states, totals, previous, grad_num, grad_den = inputs
    keep_pair = pair_mask(segment)[None]
    scores = jnp.einsum("ihm,jhm->hij", query_feat, key_feat, preferred_element_type=jnp.float32)
    masked_low = jnp.where(keep_pair, scores, 0.0).astype(jnp.bfloat16)
    reached = (segment == previous)[:, None, None]
    closing = segment[-1]
    ending = (segment == closing)[:, None, None]
    keeping = previous == closing
    grad_low = grad_states.astype(jnp.bfloat16)
    pair_grad = jnp.einsum("ihe,jhe->hij", grad_num, values, preferred_element_type=jnp.float32)
    pair_grad = pair_grad + grad_den.T[:, :, None]
    pair_low = jnp.where(keep_pair, pair_grad, 0.0).astype(jnp.bfloat16)
    query_outer = jnp.einsum(
        "ihe,hme->ihm", grad_num, states.astype(jnp.bfloat16), preferred_element_type=jnp.float32
    )
    query_outer = (
        query_outer + grad_den[:, :, None] * totals.astype(jnp.bfloat16).astype(jnp.float32)[None]
    )
    query_grad = jnp.einsum("hij,jhm->ihm", pair_low, key_feat, preferred_element_type=jnp.float32)
    query_grad = query_grad + jnp.where(reached, query_outer, 0.0)
    key_outer = (
        jnp.einsum("jhe,hme->jhm", values, grad_low, preferred_element_type=jnp.float32)
        + grad_totals[None]
    )
    key_grad = jnp.einsum("hij,ihm->jhm", pair_low, query_feat, preferred_element_type=jnp.float32)
    key_grad = key_grad + jnp.where(ending, key_outer, 0.0)
    value_outer = jnp.einsum("jhm,hme->jhe", key_feat, grad_low, preferred_element_type=jnp.float32)
    value_grad = jnp.einsum(
        "hij,ihe->jhe", masked_low, grad_num, preferred_element_type=jnp.float32
    )
    value_grad = value_grad + jnp.where(ending, value_outer, 0.0)
    reached_feat = jnp.where(reached, query_feat, jnp.zeros_like(query_feat))
    states_in = jnp.where(keeping, grad_states, 0.0) + jnp.einsum(
        "ihm,ihe->hme", reached_feat, grad_num, preferred_element_type=jnp.float32
    )
    totals_in = jnp.where(keeping, grad_totals, 0.0) + jnp.sum(
        jnp.where(reached[:, :, 0], grad_den, 0.0)[:, :, None] * query_feat, 0
    )
    return ((states_in, totals_in), (query_grad, key_grad, value_grad))


def local(
    tokens,
    cotangent,
    seq_lengths,
    features,
    ln1_gain,
    w_qkv,
    w_out,
    b_out,
    ln2_gain,
    w_in,
    b_in,
    w_down,
    b_down,
):
    row_count = tokens.shape[0]
    model_width = tokens.shape[1]
    head_count = features.shape[0]
    head_width = features.shape[1]
    feature_count = features.shape[2]
    block_rows = min(512, row_count)
    block_count = row_count // block_rows
    first_row = lax.axis_index("tensor") * row_count
    lengths = seq_lengths[0]
    offsets = jnp.cumsum(lengths) - lengths
    places = first_row + jnp.arange(row_count, dtype=jnp.int32)
    segment = jnp.sum((places[:, None] >= offsets[None, :]).astype(jnp.int32), 1) - 1
    before = jnp.sum((first_row - 1 >= offsets).astype(jnp.int32)) - 1
    flowing = tokens.astype(jnp.float32)
    scaled_one, inverse_one = normalize(flowing)
    normed_one = (scaled_one * ln1_gain).astype(jnp.bfloat16)
    mixed_qkv = jnp.dot(normed_one, w_qkv, preferred_element_type=jnp.float32)
    shrink = head_width ** (-0.25)
    head_shape = (row_count, head_count, head_width)
    query_s = (mixed_qkv[:, :model_width] * shrink).astype(jnp.bfloat16).reshape(head_shape)
    key_s = (
        (mixed_qkv[:, model_width : 2 * model_width] * shrink)
        .astype(jnp.bfloat16)
        .reshape(head_shape)
    )
    value_s = mixed_qkv[:, 2 * model_width :].astype(jnp.bfloat16).reshape(head_shape)
    query_exact, query_feat = feature_map(query_s, features, feature_count)
    key_exact, key_feat = feature_map(key_s, features, feature_count)
    closing = segment[-1]
    tail_keys = jnp.where((segment == closing)[:, None, None], key_feat, jnp.zeros_like(key_feat))
    summary = (
        jnp.einsum("jhm,jhe->hme", tail_keys, value_s, preferred_element_type=jnp.float32),
        jnp.sum(tail_keys.astype(jnp.float32), 0),
        (closing != before).astype(jnp.float32),
    )
    identity = (
        jnp.zeros((head_count, feature_count, head_width), jnp.float32),
        jnp.zeros((head_count, feature_count), jnp.float32),
        jnp.zeros((), jnp.float32),
    )
    incoming = prefix(summary, "tensor", link_states, identity, False)

    def blocked(array):
        return array.reshape((block_count, block_rows) + array.shape[1:])

    _, stored = lax.scan(
        forward_block,
        (incoming[0], incoming[1], before),
        (blocked(query_feat), blocked(key_feat), blocked(value_s), blocked(segment)),
    )
    numerator = stored[0].reshape(head_shape)
    denominator = stored[1].reshape(row_count, head_count)
    attended = (
        (numerator / denominator[:, :, None]).reshape(row_count, model_width).astype(jnp.bfloat16)
    )
    hidden = flowing + (
        jnp.dot(attended, w_out, preferred_element_type=jnp.float32) + b_out.astype(jnp.float32)
    )
    scaled_two, inverse_two = normalize(hidden)
    normed_two = (scaled_two * ln2_gain).astype(jnp.bfloat16)
    grad_out = cotangent.astype(jnp.float32)
    all_rows = lax.all_gather(normed_two, "tensor", axis=0, tiled=True)
    inner_pre = jnp.dot(all_rows, w_in, preferred_element_type=jnp.float32) + b_in.astype(
        jnp.float32
    )
    active = jax.nn.gelu(inner_pre).astype(jnp.bfloat16)
    piece = active
    mapped = lax.psum_scatter(
        jnp.dot(piece, w_down, preferred_element_type=jnp.float32).astype(jnp.bfloat16),
        "tensor",
        scatter_dimension=0,
        tiled=True,
    ).astype(jnp.float32)
    all_grads = lax.all_gather(cotangent, "tensor", axis=0, tiled=True)
    down_grad = jnp.einsum("rf,rd->fd", active, all_grads, preferred_element_type=jnp.float32)
    act_grad = jnp.einsum("rd,fd->rf", all_grads, w_down, preferred_element_type=jnp.float32)
    unit_grad = gelu_back(inner_pre, act_grad)
    in_grad = jnp.einsum("rd,rf->df", all_rows, unit_grad, preferred_element_type=jnp.float32)
    bias_grad = jnp.sum(unit_grad.astype(jnp.float32), 0)
    piece = unit_grad
    normed_grad = lax.psum_scatter(
        jnp.einsum("rf,df->rd", piece, w_in, preferred_element_type=jnp.float32),
        "tensor",
        scatter_dimension=0,
        tiled=True,
    )
    layer_out = (hidden + (mapped + b_down.astype(jnp.float32))).astype(jnp.bfloat16)
    in_grad, bias_grad, down_grad = lax.psum((in_grad, bias_grad, down_grad), "dp")
    hidden_back, gain_two_grad = normalize_back(normed_grad, ln2_gain, scaled_two, inverse_two)
    hidden_grad = grad_out + hidden_back
    branch_grad = hidden_grad.astype(jnp.bfloat16)
    out_grad = jnp.einsum("rd,re->de", attended, branch_grad, preferred_element_type=jnp.float32)
    out_bias_grad = jnp.sum(branch_grad.astype(jnp.float32), 0)
    attend_grad = jnp.einsum(
        "re,de->rd", branch_grad, w_out, preferred_element_type=jnp.float32
    ).reshape(head_shape)
    grad_num = (attend_grad / denominator[:, :, None]).astype(jnp.bfloat16)
    grad_den = -jnp.sum(attend_grad * numerator, -1) / (denominator * denominator)
    opening = segment == before
    start_feat = jnp.where(opening[:, None, None], query_feat, jnp.zeros_like(query_feat))
    returning = (
        jnp.einsum("ihm,ihe->hme", start_feat, grad_num, preferred_element_type=jnp.float32),
        jnp.sum(jnp.where(opening[:, None], grad_den, 0.0)[:, :, None] * query_feat, 0),
        summary[2],
    )
    later_grads = prefix(returning, "tensor", link_states, identity, True)
    _, back_parts = lax.scan(
        backward_block,
        (later_grads[0], later_grads[1]),
        (
            blocked(query_feat),
            blocked(key_feat),
            blocked(value_s),
            blocked(segment),
            stored[2],
            stored[3],
            stored[4],
            blocked(grad_num),
            blocked(grad_den),
        ),
        reverse=True,
    )
    feat_shape = (row_count, head_count, feature_count)
    query_arg = (back_parts[0].reshape(feat_shape) * query_exact).astype(jnp.bfloat16)
    key_arg = (back_parts[1].reshape(feat_shape) * key_exact).astype(jnp.bfloat16)
    value_grad = back_parts[2].reshape(row_count, model_width)
    query_back = jnp.einsum("rhm,hdm->rhd", query_arg, features, preferred_element_type=jnp.float32)
    query_back = query_back - query_s.astype(jnp.float32) * jnp.sum(
        query_arg.astype(jnp.float32), -1, keepdims=True
    )
    key_back = jnp.einsum("rhm,hdm->rhd", key_arg, features, preferred_element_type=jnp.float32)
    key_back = key_back - key_s.astype(jnp.float32) * jnp.sum(
        key_arg.astype(jnp.float32), -1, keepdims=True
    )
    mixed_grad = jnp.concatenate(
        [
            (query_back * shrink).reshape(row_count, model_width),
            (key_back * shrink).reshape(row_count, model_width),
            value_grad,
        ],
        1,
    ).astype(jnp.bfloat16)
    qkv_grad = jnp.einsum("rd,re->de", normed_one, mixed_grad, preferred_element_type=jnp.float32)
    normed_one_grad = jnp.einsum("re,de->rd", mixed_grad, w_qkv, preferred_element_type=jnp.float32)
    input_back, gain_one_grad = normalize_back(normed_one_grad, ln1_gain, scaled_one, inverse_one)
    input_grad = hidden_grad + input_back
    shared = lax.psum(
        (gain_one_grad, qkv_grad, out_grad, out_bias_grad, gain_two_grad, jnp.sum(grad_out, 0)),
        ("dp", "tensor"),
    )
    return (
        layer_out,
        input_grad,
        shared[0],
        shared[1],
        shared[2],
        shared[3],
        shared[4],
        in_grad,
        bias_grad,
        down_grad,
        shared[5],
    )


def solution(mesh):
    return jax.shard_map(
        local,
        mesh=mesh,
        in_specs=(
            P(("dp", "tensor"), None),
            P(("dp", "tensor"), None),
            P("dp", None),
            P(),
            P(),
            P(),
            P(),
            P(),
            P(),
            P(None, "tensor"),
            P("tensor"),
            P("tensor", None),
            P(),
        ),
        out_specs=(
            P(("dp", "tensor"), None),
            P(("dp", "tensor"), None),
            P(),
            P(),
            P(),
            P(),
            P(),
            P(None, "tensor"),
            P("tensor"),
            P("tensor", None),
            P(),
        ),
        check_vma=False,
    )
```

profile of v0, /device:TPU:0, one launch (start us, length us, event | category | flops | bytes accessed | tf_op | source)
XLA Modules:
  0.0 956.8 jit_solution(13055797893309286123)
XLA Ops:
  20.4 5.0 convert_reduce_fusion.4
  31.3 13.5 %all-reduce = f32[4]{0:T(128)S(1)} all-reduce(f32[4]{0:T(128)S(1)} %dynamic-update-slice), channel_id=1, replica_groups=mesh['dp'=8,'tensor'=4] {'tensor'}, use_global_device_ids=true, to_apply=%add | all-reduce | flops 4 | bytes 32
  47.9 2.8 copy.128
  50.7 13.7 %all-gather.1 = f32[32,256]{1,0:T(8,128)S(1)} all-gather(f32[8,256]{1,0:T(8,128)S(1)} %get-tuple-element.1059), channel_id=3, replica_groups=mesh['dp'=8,'tensor'=4] {'tensor'}, dimensions={0}, use_global_device_ids=true | all-gather | bytes 40960 | tf_op jit(solution)/shard_map/all_gather | solution.py:11
  64.7 5.5 fusion.136
  70.2 8.5 all-gather.13.cloned.1.call-done
  78.7 18.9 %while.82 = (s32[]{:T(128)}, f32[8,256,64]{2,1,0:T(8,128)}, f32[8,256]{1,0:T(8,128)S(1)}, s32[]{:T(128)}, f32[4,8,256,64]{2,3,1,0:T(8,128)}, /*index=5*/f32[4]{0...) while((s32[]{:T(128)}, f32[8,256,64]{2,1,0:T(8,128)}, ...), condition=%wide.region_8.9_spmd.clone, body=%wide.region_7.8_spmd.clone.sunk | while | flops 532485 | bytes 3694763 | solution.py:24
  99.1 68.2 %while.80 = (s32[]{:T(128)}, f32[8,256,64]{1,2,0:T(8,128)S(1)}, f32[8,256]{1,0:T(8,128)S(1)}, s32[]{:T(128)}, f32[2,512,8,64]{1,0,3,2:T(2,128)}, /*index=5*/f32[...) while((s32[]{:T(128)}, f32[8,256,64]{1,2,0:T(8,128)S(1)}, ...), condition=%wide.region_13.14_spmd, body=%wide.region_10.13_spmd.sunk | while | flops 1627006464 | bytes 74869128 | solution.py:198
  106.2 3.2 select_reduce_fusion.2
  113.0 19.6 %dynamic_update_slice.64 = f32[2,512,8,64]{1,0,3,2:T(2,128)} dynamic-update-slice(f32[2,512,8,64]{1,0,3,2:T(2,128)} %get-tuple-element.1422, f32[1,512,8,64]{1,0,3,2:T(1,128)S(1)} %copy.206, s32[]{:T(128)S(6)} %copy.239, s32[]{:T(128)} %constant.211.clone.1..sunk, s32[]{:T(128)} %constant.211.clone.1..sunk, s32[]{:T(128)} %constant.211.clone.1..sunk) | dynamic-update-slice | bytes 2097156 | tf_op jit(solution)/shard_map/while/body/jit(dynamic_update_index_in_dim)/dynamic_update_slice | solution.py:198
  140.3 3.2 select_reduce_fusion.2
  147.1 19.6 %dynamic_update_slice.64 = f32[2,512,8,64]{1,0,3,2:T(2,128)} dynamic-update-slice(f32[2,512,8,64]{1,0,3,2:T(2,128)} %get-tuple-element.1422, f32[1,512,8,64]{1,0,3,2:T(1,128)S(1)} %copy.206, s32[]{:T(128)S(6)} %copy.239, s32[]{:T(128)} %constant.211.clone.1..sunk, s32[]{:T(128)} %constant.211.clone.1..sunk, s32[]{:T(128)} %constant.211.clone.1..sunk) | dynamic-update-slice | bytes 2097156 | tf_op jit(solution)/shard_map/while/body/jit(dynamic_update_index_in_dim)/dynamic_update_slice | solution.py:198
  174.7 78.5 %all-gather.9.cloned.1.call-done = bf16[4096,512]{0,1:T(8,128)(2,1)} async-done(((bf16[1024,512]{0,1:T(8,128)(2,1)}), bf16[4096,512]{0,1:T(8,128)(2,1)}) %all-gather.9.cloned.1.call-update) | async-done | bytes 4194320 | tf_op jit(solution)/shard_map/all_gather | solution.py:214
  253.2 8.0 fusion.190
  261.2 72.9 %all-gather.11.cloned.1.call-done = bf16[4096,512]{1,0:T(8,128)(2,1)} async-done(((bf16[1024,512]{1,0:T(8,128)(2,1)}), bf16[4096,512]{1,0:T(8,128)(2,1)}) %all-gather.11.cloned.1.call-update) | async-done | bytes 4194320 | tf_op jit(solution)/shard_map/all_gather | solution.py:226
  334.1 12.8 %convert_reduce_fusion.1 = (f32[512]{0:T(512)}, bf16[4096,512]{1,0:T(8,128)(2,1)S(1)}, bf16[4096,512]{1,0:T(8,128)(2,1)}) fusion(f32[4096,512]{1,0:T(8,128)} %fusion.190, f32[512]{0:T(512)S(1)} %convert_element_type.204, bf16[4096,512]{1,0:T(8,128)(2,1)} %all-gather.11.cloned.1.call-done, bf16[512,512]{1,0:T(8,128)(2,1)S(1)} %copy-done.69), kind=kOutput, calls=%fused_computation.153 | convolution fusion | flops 2199911936 | bytes 21499904 | tf_op jit(solution)/shard_map/rd,fd->rf/dot_general | solution.py:228
  348.8 5.7 fusion.191
  354.6 6.6 convolution_convert_fusion
  363.8 4.2 reshape.375
  367.9 129.8 %reduce-scatter.5.cloned.1.call-done = f32[1024,512]{0,1:T(8,128)} async-done(((f32[4096,512]{0,1:T(8,128)}), f32[1024,512]{0,1:T(8,128)}) %reduce-scatter.5.cloned.1.call-update) | async-done | bytes 2097168 | tf_op jit(solution)/shard_map/reduce_scatter | solution.py:233
  497.7 3.5 multiply_reduce_fusion.2
  501.3 76.2 %reduce-scatter.3.cloned.1.call-done = bf16[1024,512]{0,1:T(8,128)(2,1)} async-done(((bf16[4096,512]{0,1:T(8,128)(2,1)}), bf16[1024,512]{0,1:T(8,128)(2,1)}) %reduce-scatter.3.cloned.1.call-update) | async-done | bytes 1048592 | tf_op jit(solution)/shard_map/reduce_scatter | solution.py:220
  577.4 5.5 convert_reduce_fusion.7
  588.2 6.9 fusion.193
  595.1 3.3 fusion.192
  598.5 3.3 fusion.178
  601.8 4.0 reshape.376
  605.9 3.0 multiply_reduce_fusion.1
  608.9 13.8 %all-gather.3 = f32[32,256]{1,0:T(8,128)S(1)} all-gather(f32[8,256]{1,0:T(8,128)S(1)} %multiply_reduce_fusion.1), channel_id=5, replica_groups=mesh['dp'=8,'tensor'=4] {'tensor'}, dimensions={0}, use_global_device_ids=true | all-gather | bytes 40960 | tf_op jit(solution)/shard_map/all_gather | solution.py:11
  624.1 11.1 %all-gather.15.cloned.1.call-done = f32[32,256,64]{1,2,0:T(8,128)} async-done(((f32[8,256,64]{1,2,0:T(8,128)}), f32[32,256,64]{1,2,0:T(8,128)}) %all-gather.15.cloned.1.call-update) | async-done | bytes 2097168 | tf_op jit(solution)/shard_map/all_gather | solution.py:11
  635.1 19.0 %while.83 = (s32[]{:T(128)}, f32[8,256,64]{2,1,0:T(8,128)}, f32[8,256]{1,0:T(8,128)S(1)}, s32[]{:T(128)}, f32[4,8,256,64]{2,3,1,0:T(8,128)}, /*index=5*/f32[4]{0...) while((s32[]{:T(128)}, f32[8,256,64]{2,1,0:T(8,128)}, ...), condition=%wide.region_23.24_spmd.clone, body=%wide.region_22.23_spmd.clone.sunk | while | flops 532489 | bytes 3694825 | solution.py:24
  656.8 4.1 broadcast.331.clone2
  660.9 4.2 broadcast.331.clone
  665.0 111.7 %while.81 = (s32[]{:T(128)}, f32[8,256,64]{1,2,0:T(8,128)S(1)}, f32[8,256]{1,0:T(8,128)S(1)}, f32[2,512,8,256]{3,1,0,2:T(8,128)}, f32[2,512,8,256]{3,1,0,2:T(8,1...) while((s32[]{:T(128)}, f32[8,256,64]{1,2,0:T(8,128)S(1)}, ...), condition=%wide.region_26.27_spmd, body=%wide.region_24.26_spmd.sunk | while | flops 4318831616 | bytes 160710816 | solution.py:259
  669.3 3.1 constant_dynamic-slice_fusion.11
  672.4 4.6 fusion.295
  677.0 3.2 fusion.296
  680.1 4.0 copy.207
  686.4 2.9 select_convert_fusion.14
  691.2 2.9 fusion.294
  694.2 5.4 copy.209
  701.5 5.9 fusion.291
  708.3 5.4 copy.208
  713.6 7.5 constant_dynamic-update-slice_fusion.3
  725.3 3.1 constant_dynamic-slice_fusion.11
  728.3 4.4 fusion.295
  732.8 3.2 fusion.296
  736.0 4.0 copy.207
  742.1 2.9 select_convert_fusion.14
  746.9 2.9 fusion.294
  749.9 5.3 copy.209
  757.2 5.9 fusion.291
  763.9 5.4 copy.208
  769.3 7.4 constant_dynamic-update-slice_fusion.3
  776.8 7.6 convert_reduce_fusion.3
  787.4 4.1 convert_reduce_fusion.2
  791.6 2.7 fusion.156
  798.1 3.5 fusion.167
  802.3 14.2 %psum.69 = f32[512]{0:T(512)} all-reduce(f32[512]{0:T(512)S(1)} %copy-done.62), channel_id=1, replica_groups=mesh['dp'=8,'tensor'=4] {'dp'}, use_global_device_ids=true, to_apply=%region_41.42 | all-reduce | flops 512 | bytes 4096 | tf_op jit(solution)/shard_map/psum | solution.py:240
  818.8 4.0 fusion.151
  824.9 2.9 copy.145
  827.8 38.3 %all-reduce.1 = (f32[512]{0:T(512)}, f32[512]{0:T(512)}, f32[512]{0:T(512)}, f32[512]{0:T(512)}) all-reduce(f32[512]{0:T(512)S(1)} %get-tuple-element.953, f32[512]{0:T(512)S(1)} %copy-done.60, f32[512]{0:T(512)S(1)} %copy-done.59, f32[512]{0:T(512)S(1)} %copy-done.61), channel_id=1, replica_groups=mesh['dp'=8,'tensor'=4] {'dp','tensor'}, use_global_device_ids=true, to_apply=%region_32.33 | all-reduce | flops 2048 | bytes 16384 | tf_op jit(solution)/shard_map/psum | solution.py:299
  866.1 76.6 %all-reduce.7.cloned.1.call-done = (f32[512,1536]{1,0:T(8,128)}, f32[512,512]{1,0:T(8,128)}) async-done(((f32[512,1536]{1,0:T(8,128)}, f32[512,512]{1,0:T(8,128)}), (f32[512,1536]{1,0:T(8,128)}, f32[512,512]{1,0:T(8,128)})) %all-reduce.7.cloned.1.call-update) | async-done | bytes 4194320 | tf_op jit(solution)/shard_map/psum | solution.py:299
  942.7 3.9 copy.288
  (370 shorter events, 129.5 us)
Async XLA Ops:
  7.2 71.5 %all-gather.13.cloned.1.call-start = ((), (), s32[]{:S(2)}) async-start(), calls=%async_computation.6 | async-start | bytes 2621440 | tf_op jit(solution)/shard_map/all_gather | solution.py:11
  11.4 3.1 copy-start.68
  12.5 4.1 copy-start.32
  14.5 6.0 copy-start.46
  19.4 6.0 copy-start.27
  19.7 5.7 copy-start.48
  20.4 7.1 copy-start.30
  27.5 17.3 %copy-start.31 = (bf16[1024,512]{0,1:T(8,128)(2,1)S(1)}, bf16[1024,512]{0,1:T(8,128)(2,1)}, u32[]{:S(2)}) copy-start(bf16[1024,512]{0,1:T(8,128)(2,1)} %copy.122) | copy-start | bytes 3145732
  27.5 18.9 %copy-start.65 = (bf16[512]{0:T(512)(128)(2,1)S(1)}, bf16[512]{0:T(512)(128)(2,1)}, u32[]{:S(2)}) copy-start(bf16[512]{0:T(512)(128)(2,1)} %param.28) | copy-start | bytes 3076
  29.2 224.0 %all-gather.9.cloned.1.call-start = ((), (), s32[]{:S(2)}) async-start(), calls=%async_computation.2 | async-start | bytes 5242880 | tf_op jit(solution)/shard_map/all_gather | solution.py:214
  47.9 22.2 %copy-start.17 = (bf16[1024,512]{0,1:T(8,128)(2,1)}, bf16[1024,512]{0,1:T(8,128)(2,1)S(1)}, u32[]{:S(2)}) copy-start(bf16[1024,512]{0,1:T(8,128)(2,1)S(1)} %copy.125) | copy-start | bytes 3145732
  64.7 5.5 copy-start.44
  99.1 7.0 copy-start.35
  100.5 5.6 copy-start.3
  106.2 3.2 copy-start.36
  106.2 3.2 copy-start.16
  133.3 7.0 copy-start.35
  134.6 5.6 copy-start.3
  140.3 3.2 copy-start.36
  140.3 3.2 copy-start.16
  170.9 3.8 copy-start.66
  170.9 82.3 %copy-start.38 = (bf16[512,512]{1,0:T(8,128)(2,1)S(1)}, bf16[512,512]{1,0:T(8,128)(2,1)}, u32[]{:S(2)}) copy-start(bf16[512,512]{1,0:T(8,128)(2,1)} %param.30) | copy-start | bytes 1572868
  173.4 160.7 %all-gather.11.cloned.1.call-start = ((), (), s32[]{:S(2)}) async-start(), calls=%async_computation.4 | async-start | bytes 5242880 | tf_op jit(solution)/shard_map/all_gather | solution.py:226
  174.2 323.6 %reduce-scatter.5.cloned.1.call-start = ((), (), s32[]{:S(2)}) async-start(), calls=%async_computation.5 | async-start | bytes 10485760 | tf_op jit(solution)/shard_map/reduce_scatter | solution.py:233
  174.7 159.4 %copy-start.69 = (bf16[512,512]{1,0:T(8,128)(2,1)S(1)}, bf16[512,512]{1,0:T(8,128)(2,1)}, u32[]{:S(2)}) copy-start(bf16[512,512]{1,0:T(8,128)(2,1)} %param.32) | copy-start | bytes 1572868
  354.6 222.8 %reduce-scatter.3.cloned.1.call-start = ((), (), s32[]{:S(2)}) async-start(), calls=%async_computation.3 | async-start | bytes 5242880 | tf_op jit(solution)/shard_map/reduce_scatter | solution.py:220
  361.3 273.9 %all-gather.15.cloned.1.call-start = ((), (), s32[]{:S(2)}) async-start(), calls=%async_computation.7 | async-start | bytes 2621440 | tf_op jit(solution)/shard_map/all_gather | solution.py:11
  363.8 213.6 %copy-start.34 = (bf16[1024,512]{0,1:T(8,128)(2,1)S(1)}, bf16[1024,512]{0,1:T(8,128)(2,1)}, u32[]{:S(2)}) copy-start(bf16[1024,512]{0,1:T(8,128)(2,1)} %copy.132) | copy-start | bytes 3145732
  577.4 6.8 copy-start.21
  582.9 3.4 copy-start.4
  588.1 278.0 %all-reduce.9.cloned.1.call-start = ((), (), s32[]{:S(2)}) async-start(), calls=%async_computation.9 | async-start | bytes 4194304 | tf_op jit(solution)/shard_map/psum | solution.py:240
  588.1 6.9 copy-start.23
  588.2 6.9 copy-start.25
  595.1 3.4 copy-start.29
  598.5 344.2 %all-reduce.7.cloned.1.call-start = ((), (), s32[]{:S(2)}) async-start(), calls=%async_computation.8 | async-start | bytes 8388608 | tf_op jit(solution)/shard_map/psum | solution.py:299
  605.8 16.9 %copy-start.22 = (f32[2,512,8,64]{1,0,3,2:T(2,128)S(1)}, f32[2,512,8,64]{1,0,3,2:T(2,128)}, u32[]{:S(2)}) copy-start(f32[2,512,8,64]{1,0,3,2:T(2,128)} %reshape.376) | copy-start | bytes 6291460
  665.0 111.7 %copy-start.45 = (f32[1024,8]{0,1:T(8,128)S(1)}, f32[1024,8]{0,1:T(8,128)}, u32[]{:S(2)}) copy-start(f32[1024,8]{0,1:T(8,128)} %copy-done.44) | copy-start | bytes 98308
  665.2 3.9 copy-start.52
  665.2 3.9 copy-start.72
  669.0 8.0 copy-start.50
  680.1 6.2 copy-start.15
  701.5 5.9 copy-start.8
  713.6 7.5 copy-start.53
  713.6 7.5 copy-start.73
  721.2 3.9 copy-start.52
  721.2 3.9 copy-start.72
  725.0 7.8 copy-start.50
  736.0 6.1 copy-start.15
  757.2 5.9 copy-start.8
  769.3 7.4 copy-start.53
  769.3 7.4 copy-start.73
  776.7 7.7 slice-start
  776.8 8.3 slice-start.1
  776.8 10.7 %copy-start.19 = (f32[8,1024,256]{2,1,0:T(8,128)S(1)}, f32[8,1024,256]{2,1,0:T(8,128)}, u32[]{:S(2)}) copy-start(f32[8,1024,256]{2,1,0:T(8,128)} %get-tuple-element.1080) | copy-start | bytes 25165828
  776.8 10.7 %copy-start.49 = (f32[1024,8]{0,1:T(8,128)S(1)}, f32[1024,8]{0,1:T(8,128)}, u32[]{:S(2)}) copy-start(f32[1024,8]{0,1:T(8,128)} %copy-done.48) | copy-start | bytes 98308
  787.4 4.1 copy-start.47
  791.5 4.2 copy-start.18
  818.8 4.0 copy-start.11
  822.8 5.0 copy-start.59
  822.9 4.9 copy-start.60
  822.9 4.9 copy-start.61
  942.7 3.9 copy-start.41
  942.7 4.9 copy-start.40
  942.7 5.9 copy-start.39
  (38 other events, 78.9 us)
Sparse Core Ops, SparseCore 0:
  29.3 49.2 all-gather.12
  173.6 79.5 all-gather.8
  254.8 79.2 all-gather.10
  354.7 143.0 reduce-scatter.4
  499.9 77.4 reduce-scatter.2
  588.2 46.8 all-gather.14
  638.7 60.3 all-reduce.8
  801.8 140.8 all-reduce.6
where the time goes:
time: 967 us; the launch traced here: 957 us
  waiting for transfers between devices  454 us (47%)
  local copies, waits for them, and re-layouts  178 us (18%)
  matrix products  138 us (14%)
  blocking collectives  93.5 us (10%)
  other arithmetic  64 us (7%)
  between operations  16.7 us (2%)
  loops' own time  11.6 us (1%)
    reduce_scatter x1, waiting for transfers between devices, local(): lax.psum_scatter(jnp.einsum('rf,df->rd', piece, w_in, preferred_element_t...  130 us
    all_gather x1, waiting for transfers between devices, local(): all_rows = lax.all_gather(normed_two, 'tensor', axis=0, tiled=True)  78.5 us
    psum x1, waiting for transfers between devices, local(): lax.psum((gain_one_grad, qkv_grad, out_grad, out_bias_grad, gain_two_grad...  76.6 us
    reduce_scatter x1, waiting for transfers between devices, local(): lax.psum_scatter(jnp.dot(piece, w_down, preferred_element_type=jnp.float3...  76.2 us
    all_gather x1, waiting for transfers between devices, local(): all_grads = lax.all_gather(cotangent, 'tensor', axis=0, tiled=True)  72.9 us
    dynamic_update_slice x10, local copies, waits for them, and re-layouts, local(): lax.scan(forward_block, (incoming[0], incoming[1], before), (blocked(quer...  41.7 us
    psum x1, blocking collectives, local(): lax.psum((gain_one_grad, qkv_grad, out_grad, out_bias_grad, gain_two_grad...  38.3 us
    dynamic_update_slice x6, local copies, waits for them, and re-layouts, local(): lax.scan(backward_block, (later_grads[0], later_grads[1]), (blocked(query...  36.4 us
  transfers between devices with their start and end apart: 8, of which 7 were waited for; matrix products, arithmetic and copies ran while one was open for 23% of the time, Pallas kernels for 0%

commit v1 on v0

v1 whole, which is shorter than its diff:
```python
import functools

import jax
import jax.numpy as jnp
from jax import lax
from jax.experimental import pallas as pl
from jax.experimental.pallas import tpu as pltpu
from jax.sharding import PartitionSpec as P

MESH = pl.DeviceIdType.MESH
F32 = jnp.float32
BF16 = jnp.bfloat16
EPSILON = 1e-05
BR = 256
SQRT_2_OVER_PI = 0.7978845608028654
CUBIC = 0.044715


def dot(a, b):
    return jnp.dot(a, b, preferred_element_type=F32)


def dot_rt(a, b):
    return lax.dot_general(a, b, (((1,), (1,)), ((), ())), preferred_element_type=F32)


def dot_lt(a, b):
    return lax.dot_general(a, b, (((0,), (0,)), ((), ())), preferred_element_type=F32)


def xor(a, b, size):
    out, bit = 0, 1
    while bit < size:
        out = out + bit * lax.rem(lax.div(a, bit) + (b // bit if isinstance(b, int) else lax.div(b, bit)), 2)
        bit *= 2
    return out


def iota(shape, axis):
    return lax.broadcasted_iota(jnp.int32, shape, axis)


def layer_kernel(
    tn,
    dpn,
    lens,
    tok,
    cot,
    feats,
    g1,
    wqkv,
    wout,
    bout,
    g2,
    win,
    bin_,
    wdn,
    bdn,
    layer_out,
    igrad,
    fin,
    vec_out,
    wfull,
    n1s,
    qs,
    ks,
    vs,
    phq,
    phk,
    featx,
    bsw,
    mask,
    maskt,
    lst,
    sb,
    rsw_s,
    attn,
    facc,
    xh2,
    rstd2,
    n2s,
    ad,
    chf_in,
    chf_out,
    chb_in,
    chb_out,
    gbuf,
    ra,
    rb,
    rc,
    rca,
    vec,
    va,
    vb,
    vc,
    wz_s,
    wz_r,
    wc_s,
    wc_r,
    chf_s,
    chf_r,
    chb_s,
    chb_r,
    a_s,
    a_r,
    b_s,
    b_r,
    c_s,
    c_r,
    d_s,
    d_r,
    e_s,
    e_r,
    va_s,
    va_r,
    vb_s,
    vb_r,
    vc_s,
    vc_r,
):
    rows_n, width = tok.shape
    heads, hw, feat_n = feats.shape
    pairs = heads // 2
    pw = 2 * hw
    nb = rows_n // BR
    seqs = lens.shape[1]
    shrink = hw ** (-0.25)
    featscale = feat_n ** (-0.5)
    npeer = dpn // 2
    rp = width // npeer

    dp = lax.axis_index("dp")
    t = lax.axis_index("tensor")
    cb = lax.rem(dp, 2)
    q = lax.div(dp, 2)
    core_dev = (dp + 1 - 2 * cb, t)

    def peer(k):
        return xor(q, k, npeer)

    def peer_dev(k):
        return (2 * peer(k) + cb, t)

    def z_dev(k):
        return (dp, xor(t, k, tn))

    def own_rows():
        return pl.ds(pl.multiple_of(q * rp, rp), rp)

    bar = pltpu.get_barrier_semaphore()
    targets = [core_dev] + [peer_dev(k) for k in range(1, npeer)] + [z_dev(k) for k in range(1, tn)]
    for dev in targets:
        pl.semaphore_signal(bar, inc=1, device_id=dev, device_id_type=MESH)
    pl.semaphore_wait(bar, len(targets))

    def remote(src, dst, ss, rs, dev):
        return pltpu.make_async_remote_copy(
            src_ref=src, dst_ref=dst, send_sem=ss, recv_sem=rs, device_id=dev, device_id_type=MESH
        )

    def wz_copy(k):
        return remote(wfull.at[0, cb], wfull.at[k, cb], wz_s.at[k - 1], wz_r.at[k - 1], z_dev(k))

    def wc_copy(k):
        return remote(wfull.at[k, cb], wfull.at[k, cb], wc_s.at[k - 1], wc_r.at[k - 1], core_dev)

    def chf_copy(p):
        return remote(chf_out.at[p], chf_in.at[p], chf_s.at[p], chf_r.at[p], (dp, lax.rem(t + 1, tn)))

    def chb_copy(p):
        return remote(chb_out.at[p], chb_in.at[p], chb_s.at[p], chb_r.at[p], (dp, lax.rem(t + tn - 1, tn)))

    def a_copy(s):
        s = jnp.int32(s)
        return remote(gbuf.at[s, 1 - cb], ra.at[lax.rem(s, 2)], a_s.at[s], a_r.at[s], core_dev)

    def b_copy(s, k):
        s = jnp.int32(s)
        rows = pl.ds(pl.multiple_of(peer(k) * rp, rp), rp)
        return remote(gbuf.at[s, cb, rows], rb.at[lax.rem(s, 4), k - 1], b_s.at[s, k - 1], b_r.at[s, k - 1], peer_dev(k))

    def c_copy(s):
        return remote(gbuf.at[s, cb, own_rows()], rc.at[s - 1], c_s.at[0, s - 1], c_r.at[0, s - 1], z_dev(s))

    def ca_copy(i, k):
        return remote(
            rca.at[i, 0], rca.at[i, k], c_s.at[1 + i, k - 1], c_r.at[1 + i, k - 1], z_dev(k)
        )

    def d_copy(i, k):
        here = fin.at[i, cb, own_rows()]
        return remote(here, here, d_s.at[i, k - 1], d_r.at[i, k - 1], peer_dev(k))

    def d_recv(i, k):
        rows = pl.ds(pl.multiple_of(peer(k) * rp, rp), rp)
        here = fin.at[i, cb, rows]
        return remote(here, here, d_s.at[i, k - 1], d_r.at[i, k - 1], peer_dev(k))

    def e_copy(i):
        return remote(fin.at[i, cb], fin.at[i, cb], e_s.at[i], e_r.at[i], core_dev)

    def e_recv(i):
        return remote(fin.at[i, 1 - cb], fin.at[i, 1 - cb], e_s.at[i], e_r.at[i], core_dev)

    def a_start(s):
        a_copy(s).start()

    def a_finish(s):
        s = jnp.int32(s)
        a_copy(s).wait()
        gbuf[s, cb] = (gbuf[s, cb].astype(F32) + ra[lax.rem(s, 2)].astype(F32)).astype(BF16)
        for k in range(1, npeer):
            b_copy(s, k).start()

    def b_sum(s):
        s = jnp.int32(s)
        for k in range(1, npeer):
            b_copy(s, k).wait()
        total = gbuf[s, cb, own_rows()].astype(F32)
        for k in range(1, npeer):
            total = total + rb[lax.rem(s, 4), k - 1].astype(F32)
        return total.astype(BF16)

    def b_finish(s):
        gbuf[s, cb, own_rows()] = b_sum(s)

    def c_start(s):
        c_copy(s).start()

    def c_finish():
        total = gbuf[0, cb, own_rows()].astype(F32)
        for k in range(1, tn):
            c_copy(k).wait()
            total = total + rc[k - 1].astype(F32)
        fin[0, cb, own_rows()] = total.astype(BF16)
        for k in range(1, npeer):
            d_copy(0, k).start()

    def ca_start(i):
        rca[i, 0] = b_sum(tn + i)
        for k in range(1, tn):
            ca_copy(i, k).start()

    def ca_finish(i):
        for k in range(1, tn):
            ca_copy(i, k).wait()
        total = rca[i, xor(t, 0, tn)].astype(F32)
        for j in range(1, tn):
            total = total + rca[i, xor(t, j, tn)].astype(F32)
        fin[1 + i, cb, own_rows()] = total.astype(BF16)
        for k in range(1, npeer):
            d_copy(1 + i, k).start()

    def d_finish(i):
        for k in range(1, npeer):
            d_copy(i, k).wait_send()
            d_recv(i, k).wait_recv()
        e_copy(i).start()

    def e_finish(i):
        e_copy(i).wait_send()
        e_recv(i).wait_recv()

    offsets = [jnp.int32(0)]
    for c in range(1, seqs):
        offsets.append(offsets[-1] + lens[0, c - 1])
    first = t * rows_n

    def seg_at(r):
        seg = -1
        for off in offsets:
            seg = seg + jnp.where(r >= off, 1, 0)
        return seg

    def seg_array(shape, axis, start):
        places = iota(shape, axis) + start
        seg = jnp.full(shape, -1, jnp.int32)
        for off in offsets:
            seg = seg + jnp.where(places >= off, 1, 0)
        return seg

    before = seg_at(first - 1)
    closing = seg_at(first + rows_n - 1)
    passing = jnp.where(before == closing, 1.0, 0.0)

    def prev_of(b):
        return seg_at(first + b * BR - 1)

    def last_of(b):
        return seg_at(first + b * BR + BR - 1)

    def keep_of(b):
        return jnp.where(prev_of(b) == last_of(b), 1.0, 0.0)

    def ending(b):
        return seg_array((BR, pw), 0, first + b * BR) == last_of(b)

    def reached(b):
        return seg_array((BR, pw), 0, first + b * BR) == prev_of(b)

    def block(b):
        return pl.ds(pl.multiple_of(b * BR, BR), BR)

    def lanes(p):
        return pl.ds(pl.multiple_of(p * pw, pw), pw)

    low_lane = iota((BR, pw), 1) < hw
    low_row = iota((pw, feat_n), 0) < hw
    row_id = iota((pw, feat_n), 0)

    wfull[0, 0, :width] = win[...]
    wfull[0, 0, width:] = jnp.broadcast_to(bin_[...].astype(F32), (16, bin_.shape[1])).astype(BF16)
    wfull[0, 1, :width] = wdn[...]
    wfull[0, 1, width:] = jnp.zeros((16, wdn.shape[1]), BF16)
    for k in range(1, tn):
        wz_copy(k).start()

    featx[...] = jnp.zeros_like(featx)
    for p in range(pairs):
        for o in range(2):
            featx[p, o * hw : (o + 1) * hw, o * feat_n : (o + 1) * feat_n] = feats[2 * p + o]
            for rep in (1, 2):
                featx[
                    p, rep * pw + o * hw : rep * pw + (o + 1) * hw, o * feat_n : (o + 1) * feat_n
                ] = jnp.full((hw, feat_n), -0.5, BF16)
    ri, ci = iota((2 * pw, pw), 0), iota((2 * pw, pw), 1)
    swap = (lax.rem(ri, pw) < hw) != (ci < hw)
    bsw[...] = jnp.where(swap, 1.0, 0.0).astype(BF16)

    def build_mask(b, _):
        seg_i = seg_array((BR, BR), 0, first + b * BR)
        seg_j = seg_array((BR, BR), 1, first + b * BR)
        same = seg_i == seg_j
        i, j = iota((BR, BR), 0), iota((BR, BR), 1)
        mask[b] = jnp.where(same & (i >= j), 1.0, 0.0)
        maskt[b] = jnp.where(same & (j >= i), 1.0, 0.0)
        return 0

    lax.fori_loop(0, nb, build_mask, 0)
    lst[0] = jnp.zeros(lst.shape[1:], F32)
    vec[...] = jnp.zeros_like(vec)

    @pl.when(t == 0)
    def _():
        chf_in[...] = jnp.zeros_like(chf_in)

    @pl.when(t == tn - 1)
    def _():
        chb_in[...] = jnp.zeros_like(chb_in)

    def features_of(x, p):
        wide = x.astype(F32)
        square = wide * wide
        high = square.astype(BF16)
        rest = (square - high.astype(F32)).astype(BF16)
        arg = dot(jnp.concatenate([x, high, rest], 1), featx[p])
        return (jnp.exp(arg) * featscale).astype(BF16)

    def normalized(x):
        centre = jnp.mean(x, -1, keepdims=True)
        shifted = x - centre
        inverse = lax.rsqrt(jnp.mean(shifted * shifted, -1, keepdims=True) + EPSILON)
        return shifted * inverse, inverse

    def values_of(p, b):
        wide = vs[p, block(b)].astype(F32)
        return jnp.where(low_lane, wide, 1.0), jnp.where(low_lane, 1.0, wide)

    def keys_block(b, _):
        scaled, _inv = normalized(tok[block(b)].astype(F32))
        normed = (scaled * g1[...]).astype(BF16)
        n1s[block(b)] = normed
        key = (dot(normed, wqkv[:, width : 2 * width]) * shrink).astype(BF16)
        val = dot(normed, wqkv[:, 2 * width :]).astype(BF16)
        end = ending(b)
        keep = keep_of(b)
        for p in range(pairs):
            kp = key[:, p * pw : (p + 1) * pw]
            ks[p, block(b)] = kp
            vs[p, block(b)] = val[:, p * pw : (p + 1) * pw]
            feat = features_of(kp, p)
            phk[p, block(b)] = feat
            wide = val[:, p * pw : (p + 1) * pw].astype(F32)
            even = jnp.where(end, jnp.where(low_lane, wide, 1.0), 0.0).astype(BF16)
            odd = jnp.where(end, jnp.where(low_lane, 1.0, wide), 0.0).astype(BF16)
            ue = dot_lt(even, feat[:, :feat_n])
            uo = dot_lt(odd, feat[:, feat_n:])
            lst[b + 1, p, :pw] = keep * lst[b, p, :pw] + jnp.where(low_row, ue, uo)
            lst[b + 1, p, pw : pw + 8] = keep * lst[b, p, pw : pw + 8] + ue[hw : hw + 8]
            lst[b + 1, p, pw + 8 :] = keep * lst[b, p, pw + 8 :] + uo[:8]
        return 0

    lax.fori_loop(0, nb, keys_block, 0)

    def chf_handle(p):
        @pl.when(t > 0)
        def _():
            chf_copy(p).wait_recv()

        @pl.when(t < tn - 1)
        def _():
            chf_out[p] = (lst[nb, p] + passing * chf_in[p].astype(F32)).astype(BF16)
            chf_copy(p).start()

    @pl.when(t == 0)
    def _():
        for p in range(pairs):
            chf_handle(p)

    forward_lag = jnp.minimum(2 * (t - 1), pairs)

    def forward_slot(k):
        p = k - forward_lag

        @pl.when((t > 0) & (p >= 0) & (p < pairs))
        def _():
            chf_handle(p)

    def queries_block(b, _):
        forward_slot(b)
        query = (dot(n1s[block(b)], wqkv[:, :width]) * shrink).astype(BF16)
        for p in range(pairs):
            qp = query[:, p * pw : (p + 1) * pw]
            qs[p, block(b)] = qp
            phq[p, block(b)] = features_of(qp, p)
        return 0

    lax.fori_loop(0, nb, queries_block, 0)
    for k in range(nb, pairs):
        forward_slot(k)

    def state_halves(state):
        top = state[:pw]
        even = jnp.where(low_row, top, jnp.broadcast_to(state[pw : pw + 1], top.shape)).astype(BF16)
        odd = jnp.where(low_row, jnp.broadcast_to(state[pw + 8 : pw + 9], top.shape), top).astype(BF16)
        return even, odd

    def attend_pair(p, _):
        forward_slot(pairs + p)

        @pl.when((p >= 1) & (p < tn))
        def _():
            k = jnp.maximum(p, 1)
            wz_copy(k).wait()
            wc_copy(k).start()

        incoming = chf_in[p].astype(F32)
        for b in range(nb):
            first_pass = jnp.where(before == prev_of(b), 1.0, 0.0)
            state = (lst[b, p] + first_pass * incoming).astype(BF16)
            sb[b, p] = state
            se, so = state_halves(state.astype(F32))
            reach = reached(b)
            ve, vo = values_of(p, b)
            outs = []
            for o, (val, st) in enumerate(((ve, se), (vo, so))):
                fq = phq[p, block(b), o * feat_n : (o + 1) * feat_n]
                fk = phk[p, block(b), o * feat_n : (o + 1) * feat_n]
                scores = jnp.where(mask[b] > 0, dot_rt(fq, fk), 0.0).astype(BF16)
                outs.append(
                    dot(scores, val.astype(BF16)) + jnp.where(reach, dot_rt(fq, st), 0.0)
                )
            inverse = 1.0 / jnp.where(low_lane, outs[1], outs[0])
            rsw_s[block(b), lanes(p)] = inverse
            num = jnp.where(low_lane, outs[0], outs[1])
            attn[block(b), lanes(p)] = (num * pltpu.roll(inverse, hw, 1)).astype(BF16)
        return 0

    lax.fori_loop(0, pairs, attend_pair, 0)
    for k in range(pairs, tn):
        wz_copy(k).wait()
        wc_copy(k).start()

    def hidden_block(b, _):
        h1 = tok[block(b)].astype(F32) + (dot(attn[block(b)], wout[...]) + bout[...])
        scaled, inverse = normalized(h1)
        xh2[block(b)] = scaled
        rstd2[block(b)] = inverse
        n2s[block(b)] = (scaled * g2[...]).astype(BF16)
        facc[block(b)] = h1 + bdn[...]
        return 0

    lax.fori_loop(0, nb, hidden_block, 0)

    def feed_chunk(s, _):
        @pl.when(s > 0)
        def _():
            k = jnp.maximum(s, 1)
            wc_copy(k).wait_send()
            other = wfull.at[k, 1 - cb]
            remote(other, other, wc_s.at[k - 1], wc_r.at[k - 1], core_dev).wait_recv()

        def rows_block(b, total):
            w_in = wfull[s, 0, :width]
            w_dn = wfull[s, 1, :width]
            u = dot(n2s[block(b)], w_in) + wfull[s, 0, width : width + 16].astype(F32)[:1]
            u2 = u * u
            th = jnp.tanh(u * (SQRT_2_OVER_PI + SQRT_2_OVER_PI * CUBIC * u2))
            half = 0.5 + 0.5 * th
            act = (u * half).astype(BF16)
            slope = half + (0.5 * u) * (1.0 - th * th) * (
                SQRT_2_OVER_PI + 3.0 * SQRT_2_OVER_PI * CUBIC * u2
            )
            ad[0, block(b)] = act
            facc[block(b)] += dot(act, w_dn)
            du = (slope * dot_rt(cot[block(b)], w_dn)).astype(BF16)
            ad[1, block(b)] = du
            back = dot_rt(du, w_in)

            @pl.when(s == 0)
            def _():
                igrad[block(b)] = back

            @pl.when(s > 0)
            def _():
                igrad[block(b)] += back

            return total + jnp.sum(du.astype(F32), 0, keepdims=True)

        total = lax.fori_loop(0, nb, rows_block, jnp.zeros((1, wdn.shape[0]), F32))
        vec[pl.ds(4 + s, 1)] = total

        @pl.when(s >= 1)
        def _():
            a_finish(jnp.maximum(s - 1, 0))

        @pl.when(s >= 2)
        def _():
            b_finish(jnp.maximum(s - 2, 0))

        @pl.when(s >= 3)
        def _():
            c_start(jnp.maximum(s - 2, 1))

        gbuf[s, 0] = dot_lt(n2s[...], ad[1]).astype(BF16)
        gbuf[s, 1] = dot_lt(cot[...], ad[0]).astype(BF16)
        a_start(s)
        return 0

    lax.fori_loop(0, tn, feed_chunk, 0)

    def norm_back(dn, gain, scaled, inverse):
        g = dn * gain
        inner = jnp.mean(g, -1, keepdims=True)
        cross = jnp.mean(g * scaled, -1, keepdims=True)
        return inverse * (g - inner - scaled * cross)

    lane_id = iota((BR, pw), 1)

    def branch_block(b, carry):
        gl2, gbo, gbd = carry
        layer_out[block(b)] = facc[block(b)].astype(BF16)
        dy = cot[block(b)].astype(F32)
        dn2 = igrad[block(b)]
        scaled = xh2[block(b)]
        dh1 = dy + norm_back(dn2, g2[...], scaled, rstd2[block(b)])
        igrad[block(b)] = dh1
        dob = dh1.astype(BF16)
        n2s[block(b)] = dob
        dattn = dot_rt(dob, wout[...])
        for p in range(pairs):
            da = dattn[:, p * pw : (p + 1) * pw]
            inverse = rsw_s[block(b), p * pw : (p + 1) * pw]
            dnum = da * pltpu.roll(inverse, hw, 1)
            prod = da * attn[block(b), p * pw : (p + 1) * pw].astype(F32)
            high = prod.astype(BF16)
            rest = (prod - high.astype(F32)).astype(BF16)
            dden = -dot(jnp.concatenate([high, rest], 1), bsw[...]) * inverse
            dhi = dden.astype(BF16).astype(F32)
            dlo = dden - dhi
            even = jnp.where(lane_id == hw, dhi, jnp.where(lane_id == hw + 1, dlo, 0.0))
            odd = jnp.where(lane_id == 0, dhi, jnp.where(lane_id == 1, dlo, 0.0))
            ad[0, block(b), p * pw : (p + 1) * pw] = jnp.where(low_lane, dnum, even).astype(BF16)
            ad[1, block(b), p * pw : (p + 1) * pw] = jnp.where(low_lane, odd, dnum).astype(BF16)
        return (
            gl2 + jnp.sum(dn2 * scaled, 0, keepdims=True),
            gbo + jnp.sum(dob.astype(F32), 0, keepdims=True),
            gbd + jnp.sum(dy, 0, keepdims=True),
        )

    zero_row = jnp.zeros((1, width), F32)
    gl2, gbo, gbd = lax.fori_loop(0, nb, branch_block, (zero_row,) * 3)
    vec[1:2] = gbo
    vec[2:3] = gl2
    vec[3:4] = gbd
    a_finish(tn - 1)
    for s in range(max(tn - 2, 0), tn - 1):
        b_finish(s)
        if s >= 1:
            c_start(s)
    gbuf[tn, 0] = dot_lt(attn[...], n2s[...]).astype(BF16)

    half_blocks = nb // 2

    def grad_at(j, b):
        if isinstance(b, int):
            return j, b // half_blocks, pl.ds((b % half_blocks) * BR, BR)
        rows = pl.ds(pl.multiple_of(lax.rem(b, half_blocks) * BR, BR), BR)
        return j, lax.div(b, half_blocks), rows

    def weight_grad(j):
        half = rows_n // 2
        total = dot_lt(n1s[:half], wfull[j, 0, :half])
        return (total + dot_lt(n1s[half:], wfull[j, 1, :half])).astype(BF16)

    def arg_back(darg, x, p):
        both = dot_rt(darg, featx[p, : 2 * pw])
        return (both[:, :pw] + (2.0 * x.astype(F32)) * both[:, pw:]) * shrink

    def chb_handle(p):
        @pl.when(t < tn - 1)
        def _():
            chb_copy(p).wait_recv()

        @pl.when(t > 0)
        def _():
            own = lst[nb - 1, p]
            for b in range(nb - 2, -1, -1):
                own = keep_of(b) * own + lst[b, p]
            chb_out[p] = (own + passing * chb_in[p].astype(F32)).astype(BF16)
            chb_copy(p).start()

    backward_lag = jnp.minimum(2 * (tn - 1 - t), pairs)

    def backward_slot(k):
        p = k - backward_lag

        @pl.when((p >= 0) & (p < pairs))
        def _():
            chb_handle(p)

    def query_pair(p, _):
        for b in range(nb):
            se, so = state_halves(sb[b, p].astype(F32))
            reach = reached(b)
            ve, vo = values_of(p, b)
            dargs, grads = [], []
            for o, (val, st) in enumerate(((ve, se), (vo, so))):
                dn = ad[o, block(b), lanes(p)]
                cdn = jnp.where(reach, dn.astype(F32), 0.0).astype(BF16)
                fq = phq[p, block(b), o * feat_n : (o + 1) * feat_n]
                fk = phk[p, block(b), o * feat_n : (o + 1) * feat_n]
                da = jnp.where(mask[b] > 0, dot_rt(dn, val.astype(BF16)), 0.0).astype(BF16)
                dfq = dot(da, fk) + dot(cdn, st)
                dargs.append((dfq * fq.astype(F32)).astype(BF16))
                grads.append(dot_lt(cdn, fq))
            ge, go = grads
            lst[b, p, :pw] = jnp.where(low_row, ge, go)
            lst[b, p, pw : pw + 8] = jnp.broadcast_to(ge[hw : hw + 1] + ge[hw + 1 : hw + 2], (8, feat_n))
            lst[b, p, pw + 8 :] = jnp.broadcast_to(go[0:1] + go[1:2], (8, feat_n))
            wfull[grad_at(0, b) + (lanes(p),)] = arg_back(
                jnp.concatenate(dargs, 1), qs[p, block(b)], p
            ).astype(BF16)
        backward_slot(p)

        @pl.when(p == 0)
        def _():
            b_finish(tn - 1)
            if tn > 1:
                c_start(tn - 1)

        @pl.when(p == 1)
        def _():
            c_finish()

        @pl.when(p == 3)
        def _():
            d_finish(0)

        return 0

    lax.fori_loop(0, pairs, query_pair, 0)
    gbuf[tn, 1] = weight_grad(0)
    a_start(tn)

    def key_pair(p, _):
        backward_slot(pairs + p)
        grad = chb_in[p].astype(F32)
        for b in range(nb - 1, -1, -1):
            top = grad[:pw]
            halves = []
            for o in range(2):
                dz = jnp.broadcast_to(grad[pw + 8 * o : pw + 8 * o + 1], top.shape)
                dz_hi = dz.astype(BF16).astype(F32)
                at = hw * (1 - o)
                filler = jnp.where(row_id == at, dz_hi, jnp.where(row_id == at + 1, dz - dz_hi, 0.0))
                halves.append(
                    (jnp.where(low_row, top, filler) if o == 0 else jnp.where(low_row, filler, top)).astype(BF16)
                )
            end = ending(b)
            ve, vo = values_of(p, b)
            dargs, dvs = [], []
            for o, (val, ds) in enumerate(((ve, halves[0]), (vo, halves[1]))):
                dn = ad[o, block(b), lanes(p)]
                fq = phq[p, block(b), o * feat_n : (o + 1) * feat_n]
                fk = phk[p, block(b), o * feat_n : (o + 1) * feat_n]
                at = jnp.where(maskt[b] > 0, dot_rt(fk, fq), 0.0).astype(BF16)
                dat = jnp.where(maskt[b] > 0, dot_rt(val.astype(BF16), dn), 0.0).astype(BF16)
                ev = jnp.where(end, val, 0.0).astype(BF16)
                dfk = dot(dat, fq) + dot(ev, ds)
                dargs.append((dfk * fk.astype(F32)).astype(BF16))
                dvs.append(dot(at, dn) + jnp.where(end, dot_rt(fk, ds), 0.0))
            wfull[grad_at(1, b) + (lanes(p),)] = arg_back(
                jnp.concatenate(dargs, 1), ks[p, block(b)], p
            ).astype(BF16)
            wfull[grad_at(2, b) + (lanes(p),)] = jnp.where(
                low_lane, dvs[0], dvs[1]
            ).astype(BF16)
            if b > 0:
                grad = keep_of(b) * grad + lst[b, p]

        @pl.when(p == 0)
        def _():
            a_finish(tn)

        @pl.when(p == 2)
        def _():
            ca_start(0)

        @pl.when(p == 3)
        def _():
            e_finish(0)

        return 0

    lax.fori_loop(0, pairs, key_pair, 0)

    @pl.when(t < tn - 1)
    def _():
        for p in range(pairs):
            chf_copy(p).wait_send()

    @pl.when(t > 0)
    def _():
        for p in range(pairs):
            chb_copy(p).wait_send()

    gbuf[tn + 1, 0] = weight_grad(1)
    gbuf[tn + 1, 1] = weight_grad(2)
    a_start(tn + 1)
    ca_finish(0)

    def input_block(b, gl1):
        dn1 = dot_rt(wfull[grad_at(0, b)], wqkv[:, :width])
        for j in range(1, 3):
            dn1 = dn1 + dot_rt(wfull[grad_at(j, b)], wqkv[:, j * width : (j + 1) * width])
        scaled, inverse = normalized(tok[block(b)].astype(F32))
        igrad[block(b)] += norm_back(dn1, g1[...], scaled, inverse)
        return gl1 + jnp.sum(dn1 * scaled, 0, keepdims=True)

    vec[0:1] = lax.fori_loop(0, nb, input_block, zero_row)
    va_copy = remote(vec, va, va_s, va_r, core_dev)
    va_copy.start()
    a_finish(tn + 1)
    d_finish(1)
    va_copy.wait()
    vb[0] = vec[...] + va[...]
    vb_copies = [remote(vb.at[0], vb.at[k], vb_s.at[k - 1], vb_r.at[k - 1], peer_dev(k)) for k in range(1, npeer)]
    for copy in vb_copies:
        copy.start()
    ca_start(1)
    for copy in vb_copies:
        copy.wait()
    total = vb[xor(q, 0, npeer)]
    for j in range(1, npeer):
        total = total + vb[xor(q, j, npeer)]
    vc[0] = total
    vc_copies = [remote(vc.at[0], vc.at[k], vc_s.at[k - 1], vc_r.at[k - 1], z_dev(k)) for k in range(1, tn)]
    for copy in vc_copies:
        copy.start()
    ca_finish(1)
    for copy in vc_copies:
        copy.wait()
    total = vc[xor(t, 0, tn)]
    for j in range(1, tn):
        total = total + vc[xor(t, j, tn)]
    own = vc[0, 4:5]
    for k in range(1, tn):
        own = own + vc[k, 4 + k : 5 + k]
    vec_out[...] = total
    vec_out[4:5] = own
    e_finish(1)
    d_finish(2)
    e_finish(2)


def local(
    tn,
    dpn,
    tokens,
    cotangent,
    seq_lengths,
    features,
    ln1_gain,
    w_qkv,
    w_out,
    b_out,
    ln2_gain,
    w_in,
    b_in,
    w_down,
    b_down,
):
    rows_n, width = tokens.shape
    heads, hw, feat_n = features.shape
    pairs, pw, nb = heads // 2, 2 * hw, rows_n // BR
    ffl = w_in.shape[1]
    npeer = dpn // 2
    rp = width // npeer
    vrows = -(-(4 + tn) // 8) * 8
    dma = pltpu.SemaphoreType.DMA
    vmem = pl.BlockSpec(memory_space=pltpu.VMEM)

    def scratch(shape, dtype=BF16):
        return pltpu.VMEM(shape, dtype)

    out = pl.pallas_call(
        functools.partial(layer_kernel, tn, dpn),
        out_shape=(
            jax.ShapeDtypeStruct((rows_n, width), BF16),
            jax.ShapeDtypeStruct((rows_n, width), F32),
            jax.ShapeDtypeStruct((3, 2, width, width), BF16),
            jax.ShapeDtypeStruct((vrows, width), F32),
        ),
        in_specs=[pl.BlockSpec(memory_space=pltpu.SMEM)] + [vmem] * 12,
        out_specs=(vmem,) * 4,
        scratch_shapes=[
            scratch((tn, 2, width + 16, ffl)),
            scratch((rows_n, width)),
            scratch((pairs, rows_n, pw)),
            scratch((pairs, rows_n, pw)),
            scratch((pairs, rows_n, pw)),
            scratch((pairs, rows_n, 2 * feat_n)),
            scratch((pairs, rows_n, 2 * feat_n)),
            scratch((pairs, 3 * pw, 2 * feat_n)),
            scratch((2 * pw, pw)),
            scratch((nb, BR, BR), F32),
            scratch((nb, BR, BR), F32),
            scratch((nb + 1, pairs, pw + 16, feat_n), F32),
            scratch((nb, pairs, pw + 16, feat_n)),
            scratch((rows_n, width), F32),
            scratch((rows_n, width)),
            scratch((rows_n, width), F32),
            scratch((rows_n, width), F32),
            scratch((rows_n, 1), F32),
            scratch((rows_n, width)),
            scratch((2, rows_n, width)),
            scratch((pairs, pw + 16, feat_n)),
            scratch((pairs, pw + 16, feat_n)),
            scratch((pairs, pw + 16, feat_n)),
            scratch((pairs, pw + 16, feat_n)),
            scratch((tn + 2, 2, width, width)),
            scratch((2, width, width)),
            scratch((4, npeer - 1, rp, width)),
            scratch((tn - 1, rp, width)),
            scratch((2, tn, rp, width)),
            scratch((vrows, width), F32),
            scratch((vrows, width), F32),
            scratch((npeer, vrows, width), F32),
            scratch((tn, vrows, width), F32),
            dma((tn - 1,)),
            dma((tn - 1,)),
            dma((tn - 1,)),
            dma((tn - 1,)),
            dma((pairs,)),
            dma((pairs,)),
            dma((pairs,)),
            dma((pairs,)),
            dma((tn + 2,)),
            dma((tn + 2,)),
            dma((tn + 2, npeer - 1)),
            dma((tn + 2, npeer - 1)),
            dma((3, tn - 1)),
            dma((3, tn - 1)),
            dma((3, npeer - 1)),
            dma((3, npeer - 1)),
            dma((3,)),
            dma((3,)),
            dma(()),
            dma(()),
            dma((npeer - 1,)),
            dma((npeer - 1,)),
            dma((tn - 1,)),
            dma((tn - 1,)),
        ],
        compiler_params=pltpu.CompilerParams(
            collective_id=0, has_side_effects=True, vmem_limit_bytes=63 * 1024 * 1024
        ),
    )(
        seq_lengths,
        tokens,
        cotangent,
        features,
        ln1_gain[None],
        w_qkv,
        w_out,
        b_out.astype(F32)[None],
        ln2_gain[None],
        w_in,
        b_in[None],
        w_down,
        b_down.astype(F32)[None],
    )
    layer_out, input_grad, fin, vec = out
    fin = fin.astype(F32)
    return (
        layer_out,
        input_grad,
        vec[0],
        jnp.concatenate([fin[1, 1], fin[2, 0], fin[2, 1]], 1),
        fin[1, 0],
        vec[1],
        vec[2],
        fin[0, 0],
        vec[4],
        fin[0, 1].T,
        vec[3],
    )


def solution(mesh):
    tn, dpn = mesh.shape["tensor"], mesh.shape["dp"]
    rows = P(("dp", "tensor"), None)
    return jax.shard_map(
        functools.partial(local, tn, dpn),
        mesh=mesh,
        in_specs=(
            rows,
            rows,
            P("dp", None),
            P(),
            P(),
            P(),
            P(),
            P(),
            P(),
            P(None, "tensor"),
            P("tensor"),
            P("tensor", None),
            P(),
        ),
        out_specs=(
            rows,
            rows,
            P(),
            P(),
            P(),
            P(),
            P(),
            P(None, "tensor"),
            P("tensor"),
            P("tensor", None),
            P(),
        ),
        check_vma=False,
    )
```

time: 967 us -> 187 us (0.19)
  waiting for transfers between devices: 454 us -> 0 us
  local copies, waits for them, and re-layouts: 178 us -> 8.35 us
  Pallas kernels: 0 us -> 168 us
  matrix products: 138 us -> 0 us
  blocking collectives: 93.5 us -> 0 us
  other arithmetic: 64 us -> 8.51 us
  between operations: 16.7 us -> 0.66 us
  loops' own time: 11.6 us -> 0 us
    reduce_scatter x2 -> x0, waiting for transfers between devices: 206 us -> none  [the longest x1 130 us: local(): lax.psum_scatter(jnp.einsum('rf,df->rd', piece, w_in, preferred_element_t...]
    all_gather x4 -> x0, waiting for transfers between devices: 171 us -> none  [the longest x1 78.5 us: local(): all_rows = lax.all_gather(normed_two, 'tensor', axis=0, tiled=True)]
    pallas_call x0 -> x1, Pallas kernels: none -> 168 us  [local(): pl.pallas_call(functools.partial(layer_kernel, tn, dpn), out_shape=(jax.S...]
    dot_general x44 -> x0, matrix products: 138 us -> none  [the longest x1 12.8 us: local(): jnp.einsum('rd,fd->rf', all_grads, w_down, preferred_element_type=jnp.flo...]
    dynamic_update_slice x16 -> x0, local copies, waits for them, and re-layouts: 78.1 us -> none  [the longest x10 41.7 us: local(): lax.scan(forward_block, (incoming[0], incoming[1], before), (blocked(quer...]
    psum x2 -> x0, waiting for transfers between devices: 76.6 us -> none  [the longest x1 76.6 us: local(): lax.psum((gain_one_grad, qkv_grad, out_grad, out_bias_grad, gain_two_grad...]
    psum x2 -> x0, blocking collectives: 52.5 us -> none  [the longest x1 38.3 us: local(): lax.psum((gain_one_grad, qkv_grad, out_grad, out_bias_grad, gain_two_grad...]
    reduce_sum x16 -> x0, other arithmetic: 34.5 us -> none  [the longest x1 7.63 us: local(): jnp.sum(query_arg.astype(jnp.float32), -1, keepdims=True)]
  transfers between devices with their start and end apart: 8 -> 0, of which waited for: 7 -> 0; matrix products, arithmetic and copies ran while one was open for 23% -> 0% of each run, Pallas kernels for 0% -> 0%
where the time goes in v1:
time: 187 us; the launch traced here: 186 us
  Pallas kernels  168 us (90%)
  other arithmetic  8.51 us (5%)
  local copies, waits for them, and re-layouts  8.35 us (4%)
    pallas_call x1, Pallas kernels, local(): pl.pallas_call(functools.partial(layer_kernel, tn, dpn), out_shape=(jax.S...  168 us

profile of v1, /device:TPU:0, one launch (start us, length us, event | category | flops | bytes accessed | tf_op | source)
XLA Modules:
  0.0 185.9 jit_solution(10765750178971619087)
XLA Ops:
  0.6 1.3 broadcast_in_dim.26
  1.9 1.3 broadcast_in_dim.23.bin_
  3.2 1.3 broadcast_in_dim.27
  4.4 168.4 %shard_map.212 = (bf16[1024,512]{1,0:T(8,128)(2,1)}, f32[1024,512]{1,0:T(8,128)}, bf16[3,2,512,512]{3,2,1,0:T(8,128)(2,1)}, f32[8,512]{1,0:T(8,128)}) custom-call(s32[1,2]{1,0:T(1,128)} %lens.1, bf16[1024,512]{1,0:T(8,128)(2,1)} %tok.1, bf16[1024,512]{1,0:T(8,128)(2,1)} %cot.1, bf16[8,64,256]{2,1,0:T(8,128)(2,1)} %feats.1, f32[1,512]{1,0:T(1,128)} %bitcast.25, ...), custom_call_target="tpu_custom_call" | custom-call | tf_op jit(solution)/shard_map/pallas_call | solution.py:817
  172.8 1.5 fusion
  174.3 2.8 %convert_element_type.2 = f32[3,2,512,512]{3,2,1,0:T(8,128)S(1)} convert(bf16[3,2,512,512]{3,2,1,0:T(8,128)(2,1)} %get-tuple-element.18) | non-fusion elementwise | flops 1572864 | bytes 9437184 | tf_op jit(solution)/shard_map/convert_element_type | solution.py:905
  177.1 2.0 %slice_bitcast_fusion = (f32[512,512]{0,1:T(8,128)S(1)}, f32[512,512]{1,0:T(8,128)}, f32[512,512]{1,0:T(8,128)}, f32[512,512]{1,0:T(8,128)S(1)}, f32[512,512]{1,0:T(8,128)S(1)}, /*index=5*/f32[512,512]{1,0:T(8,128)}) fusion(f32[3,2,512,512]{3,2,1,0:T(8,128)S(1)} %convert_element_type.2), kind=kLoop, calls=%fused_computation.1 | loop fusion | bytes 12582912 | tf_op jit(solution)/shard_map/transpose | solution.py:916
  179.1 1.3 copy.24
  180.4 0.0 copy-start.1
  180.4 0.0 copy-start
  180.4 3.2 %pad_maximum_fusion = f32[512,1536]{1,0:T(8,128)} fusion(f32[512,512]{1,0:T(8,128)S(1)} %get-tuple-element.33, f32[512,512]{1,0:T(8,128)S(1)} %get-tuple-element.34, f32[512,512]{1,0:T(8,128)} %get-tuple-element.35), kind=kLoop, calls=%fused_computation | loop fusion | flops 1572864 | bytes 6291456 | tf_op jit(solution)/shard_map/concatenate | solution.py:910
  183.6 0.0 copy-done.1
  183.6 1.0 copy.27
  184.6 0.0 copy-done
  184.6 1.3 copy.28
Async XLA Ops:
  180.4 3.2 %copy-start.1 = (bf16[1024,512]{1,0:T(8,128)(2,1)S(1)}, bf16[1024,512]{1,0:T(8,128)(2,1)}, u32[]{:S(2)}) copy-start(bf16[1024,512]{1,0:T(8,128)(2,1)} %get-tuple-element.52) | copy-start | bytes 3145732
  180.4 4.2 %copy-start = (f32[1024,512]{1,0:T(8,128)S(1)}, f32[1024,512]{1,0:T(8,128)}, u32[]{:S(2)}) copy-start(f32[1024,512]{1,0:T(8,128)} %get-tuple-element.53) | copy-start | bytes 6291460

commit v2 on v1

v2 whole, which is shorter than its diff:
```python
import functools

import jax
import jax.numpy as jnp
from jax import lax
from jax.experimental import pallas as pl
from jax.experimental.pallas import tpu as pltpu
from jax.sharding import PartitionSpec as P

MESH = pl.DeviceIdType.MESH
F32 = jnp.float32
BF16 = jnp.bfloat16
EPSILON = 1e-05
BR = 256
WR = 512
SQRT_2_OVER_PI = 0.7978845608028654
CUBIC = 0.044715


def dot(a, b):
    return jnp.dot(a, b, preferred_element_type=F32)


def dot_rt(a, b):
    return lax.dot_general(a, b, (((1,), (1,)), ((), ())), preferred_element_type=F32)


def dot_lt(a, b):
    return lax.dot_general(a, b, (((0,), (0,)), ((), ())), preferred_element_type=F32)


def xor(a, b, size):
    out, bit = 0, 1
    while bit < size:
        out = out + bit * lax.rem(lax.div(a, bit) + (b // bit if isinstance(b, int) else lax.div(b, bit)), 2)
        bit *= 2
    return out


def iota(shape, axis):
    return lax.broadcasted_iota(jnp.int32, shape, axis)


def layer_kernel(
    tn,
    dpn,
    lens,
    tok_h,
    cot_h,
    feats_h,
    g1,
    wqkv_h,
    wout_h,
    biases,
    g2,
    win_h,
    wdn_h,
    layer_h,
    igrad_h,
    fin,
    fink,
    vec_out,
    tok,
    cot,
    feats,
    wqkv,
    wout,
    layer_out,
    igrad,
    wfull,
    bfull,
    n1s,
    qs,
    ks,
    vs,
    phq,
    phk,
    featx,
    bsw,
    mask,
    maskt,
    lst,
    sb,
    rsw_s,
    attn,
    facc,
    xh2,
    rstd2,
    n2s,
    ad,
    chf_in,
    chf_out,
    chb_in,
    chb_out,
    gbuf,
    ra,
    rb,
    rc,
    kbuf,
    kra,
    krb,
    krc,
    vec,
    va,
    vb,
    vc,
    in_s,
    out_s,
    bz_s,
    bz_r,
    wz_s,
    wz_r,
    wx_s,
    wx_r,
    wc_s,
    wc_r,
    chf_s,
    chf_r,
    chb_s,
    chb_r,
    a_s,
    a_r,
    b_s,
    b_r,
    c_s,
    c_r,
    d_s,
    d_r,
    e_s,
    e_r,
    ka_s,
    ka_r,
    kb_s,
    kb_r,
    kc_s,
    kc_r,
    kd_s,
    kd_r,
    ke_s,
    ke_r,
    va_s,
    va_r,
    vb_s,
    vb_r,
    vc_s,
    vc_r,
):
    rows_n, width = tok.shape
    heads, hw, feat_n = feats.shape
    pairs = heads // 2
    pw = 2 * hw
    nb = rows_n // BR
    seqs = lens.shape[1]
    shrink = hw ** (-0.25)
    featscale = feat_n ** (-0.5)
    npeer = dpn // 2
    rp = width // npeer

    dp = lax.axis_index("dp")
    t = lax.axis_index("tensor")
    cb = lax.rem(dp, 2)
    q = lax.div(dp, 2)
    core_dev = (dp + 1 - 2 * cb, t)

    peers = [xor(q, k, npeer) for k in range(npeer)]
    zs = [xor(t, k, tn) for k in range(tn)]

    def peer_dev(k):
        return (2 * peers[k] + cb, t)

    def z_dev(k):
        return (dp, zs[k])

    row_starts = [pl.multiple_of(peer * rp, rp) for peer in peers]

    def own_rows():
        return pl.ds(row_starts[0], rp)

    def peer_rows(k):
        return pl.ds(row_starts[k], rp)

    def load(i, src, dst):
        return pltpu.make_async_copy(src, dst, in_s.at[i])

    loads = {
        "win": load(0, win_h, wfull.at[0, 0]),
        "wdn": load(1, wdn_h, wfull.at[0, 1]),
        "tok": load(2, tok_h, tok),
        "wqkv": load(3, wqkv_h, wqkv),
        "feats": load(4, feats_h, feats),
        "wout": load(5, wout_h, wout),
        "cot": load(6, cot_h, cot),
    }
    for copy in loads.values():
        copy.start()

    def store_layer():
        return pltpu.make_async_copy(layer_out, layer_h, out_s.at[0])

    def store_grad(b):
        rows = pl.ds(pl.multiple_of(b * WR, WR), WR)
        return pltpu.make_async_copy(igrad.at[rows], igrad_h.at[rows], out_s.at[1 + b])

    bar = pltpu.get_barrier_semaphore()
    targets = [core_dev] + [peer_dev(k) for k in range(1, npeer)] + [z_dev(k) for k in range(1, tn)]
    for dev in targets:
        pl.semaphore_signal(bar, inc=1, device_id=dev, device_id_type=MESH)

    def remote(src, dst, ss, rs, dev):
        return pltpu.make_async_remote_copy(
            src_ref=src, dst_ref=dst, send_sem=ss, recv_sem=rs, device_id=dev, device_id_type=MESH
        )

    def bz_copy(k):
        return remote(bfull.at[0], bfull.at[k], bz_s.at[k - 1], bz_r.at[k - 1], z_dev(k))

    def wz_copy(k):
        return remote(
            wfull.at[0, cb, own_rows()], wfull.at[k, cb, own_rows()], wz_s.at[k - 1], wz_r.at[k - 1], z_dev(k)
        )

    def wx_copy(k, j):
        here = wfull.at[k, cb, own_rows()]
        return remote(here, here, wx_s.at[k - 1, j - 1], wx_r.at[k - 1, j - 1], peer_dev(j))

    def wx_recv(k, j):
        here = wfull.at[k, cb, peer_rows(j)]
        return remote(here, here, wx_s.at[k - 1, j - 1], wx_r.at[k - 1, j - 1], peer_dev(j))

    def wc_copy(k):
        return remote(wfull.at[k, cb], wfull.at[k, cb], wc_s.at[k - 1], wc_r.at[k - 1], core_dev)

    def wc_recv(k):
        here = wfull.at[k, 1 - cb]
        return remote(here, here, wc_s.at[k - 1], wc_r.at[k - 1], core_dev)

    def w_spread(k):
        wz_copy(k).wait()
        for j in range(1, npeer):
            wx_copy(k, j).start()

    def w_swap(k):
        for j in range(1, npeer):
            wx_copy(k, j).wait_send()
            wx_recv(k, j).wait_recv()
        wc_copy(k).start()

    levels = (tn - 1).bit_length()
    up_first = (1, 3, 5, 8), (9, 11, 14, 16)

    def up_due(at, p):
        return up_first[at - 1][p % 4] if at < 3 and p < 4 else 14 + p

    def down_due(hops, p):
        due = min(3 * hops + p, 8 + 2 * p)
        return due + due % 2 if due > 8 else due

    def up_copy(p):
        return remote(chf_out.at[p], chf_in.at[p], chf_s.at[p], chf_r.at[p], (dp, lax.rem(t + 1, tn)))

    def up_handle(p):
        @pl.when(t > 0)
        def _():
            up_copy(p).wait_recv()

        chf_out[p] = (lst[nb, p] + passing * chf_in[p].astype(F32)).astype(BF16)
        up_copy(p).start()

    def up_slots(k, low, high):
        for at in range(1, tn - 1):
            for p in range(pairs):
                if low <= up_due(at, p) < high:

                    @pl.when((t == at) & (k == up_due(at, p)))
                    def _(p=p):
                        up_handle(p)

    def down_copy(p):
        return remote(chb_out.at[p], chb_in.at[p], chb_s.at[p], chb_r.at[p], (dp, lax.rem(t + tn - 1, tn)))

    def down_handle(p):
        @pl.when(t < tn - 1)
        def _():
            down_copy(p).wait_recv()

        own = lst[nb - 1, p]
        for b in range(nb - 2, -1, -1):
            own = keep_of(b) * own + lst[b, p]
        chb_out[p] = (own + passing * chb_in[p].astype(F32)).astype(BF16)
        down_copy(p).start()

    def down_slots(k, low, high):
        for hops in range(tn - 1):
            for p in range(pairs):
                if low <= down_due(hops, p) < high:

                    @pl.when((t == tn - 1 - hops) & (k == down_due(hops, p)))
                    def _(p=p):
                        down_handle(p)

    def a_copy(s):
        s = jnp.int32(s)
        return remote(gbuf.at[s, 1 - cb], ra.at[lax.rem(s, 2)], a_s.at[s], a_r.at[s], core_dev)

    def b_copy(s, k):
        s = jnp.int32(s)
        return remote(gbuf.at[s, cb, peer_rows(k)], rb.at[lax.rem(s, 4), k - 1], b_s.at[s, k - 1], b_r.at[s, k - 1], peer_dev(k))

    def c_copy(s):
        return remote(gbuf.at[s, cb, own_rows()], rc.at[s - 1], c_s.at[s - 1], c_r.at[s - 1], z_dev(s & -s))

    def d_copy(k):
        here = fin.at[cb, own_rows()]
        return remote(here, here, d_s.at[k - 1], d_r.at[k - 1], peer_dev(k))

    def d_recv(k):
        here = fin.at[cb, peer_rows(k)]
        return remote(here, here, d_s.at[k - 1], d_r.at[k - 1], peer_dev(k))

    def e_copy():
        return remote(fin.at[cb], fin.at[cb], e_s, e_r, core_dev)

    def e_recv():
        return remote(fin.at[1 - cb], fin.at[1 - cb], e_s, e_r, core_dev)

    def ka_copy(i):
        i = jnp.int32(i)
        return remote(kbuf.at[i, 1 - cb], kra.at[lax.rem(i, 4)], ka_s.at[i], ka_r.at[i], core_dev)

    def kb_copy(i, k):
        return remote(
            kbuf.at[i, cb, peer_rows(k)], krb.at[i, k - 1], kb_s.at[i, k - 1], kb_r.at[i, k - 1], peer_dev(k)
        )

    def kc_copy(i, k):
        return remote(krc.at[i, 0], krc.at[i, k], kc_s.at[i, k - 1], kc_r.at[i, k - 1], z_dev(k))

    def ks_copy(i, l):
        return remote(
            krc.at[i, 2 * l], krc.at[i, 2 * l + 1], kc_s.at[i, l], kc_r.at[i, l], z_dev(1 << l)
        )

    def kd_copy(i, k):
        here = fink.at[i, cb, own_rows()]
        return remote(here, here, kd_s.at[i, k - 1], kd_r.at[i, k - 1], peer_dev(k))

    def kd_recv(i, k):
        here = fink.at[i, cb, peer_rows(k)]
        return remote(here, here, kd_s.at[i, k - 1], kd_r.at[i, k - 1], peer_dev(k))

    def ke_copy(i):
        return remote(fink.at[i, cb], fink.at[i, cb], ke_s.at[i], ke_r.at[i], core_dev)

    def ke_recv(i):
        return remote(fink.at[i, 1 - cb], fink.at[i, 1 - cb], ke_s.at[i], ke_r.at[i], core_dev)

    def a_start(s):
        a_copy(s).start()

    def a_finish(s):
        s = jnp.int32(s)
        a_copy(s).wait()
        gbuf[s, cb] = (gbuf[s, cb].astype(F32) + ra[lax.rem(s, 2)].astype(F32)).astype(BF16)
        for k in range(1, npeer):
            b_copy(s, k).start()

    def b_sum(s):
        s = jnp.int32(s)
        for k in range(1, npeer):
            b_copy(s, k).wait()
        total = gbuf[s, cb, own_rows()].astype(F32)
        for k in range(1, npeer):
            total = total + rb[lax.rem(s, 4), k - 1].astype(F32)
        return total.astype(BF16)

    def b_finish(s):
        gbuf[s, cb, own_rows()] = b_sum(s)

    def c_add(s):
        step = 1
        while step < (s & -s if s else tn):
            c_copy(s + step).wait()
            gbuf[s, cb, own_rows()] = (
                gbuf[s, cb, own_rows()].astype(F32) + rc[s + step - 1].astype(F32)
            ).astype(BF16)
            step *= 2

    def c_start(s):
        c_add(s)
        c_copy(s).start()

    def c_finish():
        total = gbuf[0, cb, own_rows()].astype(F32)
        step = 1
        while step < tn:
            c_copy(step).wait()
            total = total + rc[step - 1].astype(F32)
            step *= 2
        fin[cb, own_rows()] = total.astype(BF16)
        for k in range(1, npeer):
            d_copy(k).start()

    def d_finish():
        for k in range(1, npeer):
            d_copy(k).wait_send()
            d_recv(k).wait_recv()
        e_copy().start()

    def e_finish():
        e_copy().wait_send()
        e_recv().wait_recv()

    def k_a_start(i, both):
        kbuf[i, 0] = both[:, :pw].astype(BF16)
        kbuf[i, 1] = both[:, pw:].astype(BF16)
        ka_copy(i).start()

    def k_a_finish(i):
        i = jnp.int32(i)
        ka_copy(i).wait()
        kbuf[i, cb] = (kbuf[i, cb].astype(F32) + kra[lax.rem(i, 4)].astype(F32)).astype(BF16)
        for k in range(1, npeer):
            kb_copy(i, k).start()

    def k_b_sum(i):
        for k in range(1, npeer):
            kb_copy(i, k).wait()
        total = kbuf[i, cb, own_rows()].astype(F32)
        for k in range(1, npeer):
            total = total + krb[i, k - 1].astype(F32)
        krc[i, 0] = total.astype(BF16)

    def k_spread(i, total):
        fink[i, cb, own_rows()] = total.astype(BF16)
        for k in range(1, npeer):
            kd_copy(i, k).start()

    def k_b_finish(i):
        k_b_sum(i)
        for k in range(1, tn):
            kc_copy(i, k).start()

    def k_c_finish(i):
        for k in range(1, tn):
            kc_copy(i, k).wait()
        total = krc[i, zs[0]].astype(F32)
        for j in range(1, tn):
            total = total + krc[i, zs[j]].astype(F32)
        k_spread(i, total)

    def s_b_finish(i):
        k_b_sum(i)
        ks_copy(i, 0).start()

    def s_sum(i, l):
        ks_copy(i, l).wait()
        return krc[i, 2 * l].astype(F32) + krc[i, 2 * l + 1].astype(F32)

    def s_middle(i):
        for l in range(levels - 1):
            krc[i, 2 * l + 2] = s_sum(i, l).astype(BF16)
            ks_copy(i, l + 1).start()

    def s_c_finish(i):
        k_spread(i, s_sum(i, levels - 1))

    def k_d_finish(i):
        for k in range(1, npeer):
            kd_copy(i, k).wait_send()
            kd_recv(i, k).wait_recv()
        ke_copy(i).start()

    def k_e_finish(i):
        ke_copy(i).wait_send()
        ke_recv(i).wait_recv()

    offsets = [jnp.int32(0)]
    for c in range(1, seqs):
        offsets.append(offsets[-1] + lens[0, c - 1])
    first = t * rows_n

    def seg_at(r):
        seg = -1
        for off in offsets:
            seg = seg + jnp.where(r >= off, 1, 0)
        return seg

    def seg_array(shape, axis, start):
        places = iota(shape, axis) + start
        seg = jnp.full(shape, -1, jnp.int32)
        for off in offsets:
            seg = seg + jnp.where(places >= off, 1, 0)
        return seg

    before = seg_at(first - 1)
    closing = seg_at(first + rows_n - 1)
    passing = jnp.where(before == closing, 1.0, 0.0)

    def prev_of(b):
        return seg_at(first + b * BR - 1)

    def last_of(b):
        return seg_at(first + b * BR + BR - 1)

    def keep_of(b):
        return jnp.where(prev_of(b) == last_of(b), 1.0, 0.0)

    def ending(b):
        return seg_array((BR, pw), 0, first + b * BR) == last_of(b)

    def reached(b):
        return seg_array((BR, pw), 0, first + b * BR) == prev_of(b)

    def block(b):
        return pl.ds(pl.multiple_of(b * BR, BR), BR)

    nw = rows_n // WR

    def wide(b):
        return pl.ds(pl.multiple_of(b * WR, WR), WR)

    def lanes(p):
        return pl.ds(pl.multiple_of(p * pw, pw), pw)

    low_lane = iota((BR, pw), 1) < hw
    low_row = iota((pw, feat_n), 0) < hw
    row_id = iota((pw, feat_n), 0)

    loads["feats"].wait()
    featx[...] = jnp.zeros_like(featx)
    for p in range(pairs):
        for o in range(2):
            featx[p, o * hw : (o + 1) * hw, o * feat_n : (o + 1) * feat_n] = feats[2 * p + o]
            for rep in (1, 2):
                featx[
                    p, rep * pw + o * hw : rep * pw + (o + 1) * hw, o * feat_n : (o + 1) * feat_n
                ] = jnp.full((hw, feat_n), -0.5, BF16)
    ri, ci = iota((2 * pw, pw), 0), iota((2 * pw, pw), 1)
    swap = (lax.rem(ri, pw) < hw) != (ci < hw)
    bsw[...] = jnp.where(swap, 1.0, 0.0).astype(BF16)

    def build_mask(b, _):
        seg_i = seg_array((BR, BR), 0, first + b * BR)
        seg_j = seg_array((BR, BR), 1, first + b * BR)
        same = seg_i == seg_j
        i, j = iota((BR, BR), 0), iota((BR, BR), 1)
        mask[b] = jnp.where(same & (i >= j), 1.0, 0.0).astype(BF16)
        maskt[b] = jnp.where(same & (j >= i), 1.0, 0.0).astype(BF16)
        return 0

    lax.fori_loop(0, nb, build_mask, 0)
    lst[0] = jnp.zeros(lst.shape[1:], F32)
    vec[...] = jnp.zeros_like(vec)

    @pl.when(t == 0)
    def _():
        chf_in[...] = jnp.zeros_like(chf_in)

    @pl.when(t == tn - 1)
    def _():
        chb_in[...] = jnp.zeros_like(chb_in)

    loads["win"].wait()
    loads["wdn"].wait()
    pl.semaphore_wait(bar, len(targets))
    bfull[0] = jnp.broadcast_to(biases[1:2], bfull.shape[1:])
    for k in range(1, tn):
        bz_copy(k).start()
    wz_copy(1).start()
    wz_copy(2).start()

    def features_of(x, p):
        wide = x.astype(F32)
        square = wide * wide
        high = square.astype(BF16)
        rest = (square - high.astype(F32)).astype(BF16)
        arg = dot(jnp.concatenate([x, high, rest], 1), featx[p])
        return (jnp.exp(arg) * featscale).astype(BF16)

    def normalized(x):
        centre = jnp.mean(x, -1, keepdims=True)
        shifted = x - centre
        inverse = lax.rsqrt(jnp.mean(shifted * shifted, -1, keepdims=True) + EPSILON)
        return shifted * inverse, inverse

    def values_of(p, b):
        wide = vs[p, block(b)].astype(F32)
        return jnp.where(low_lane, wide, 1.0), jnp.where(low_lane, 1.0, wide)

    def keys_block(b, _):
        scaled, _inv = normalized(tok[wide(b)].astype(F32))
        normed = (scaled * g1[...]).astype(BF16)
        n1s[wide(b)] = normed
        key = (dot(normed, wqkv[:, width : 2 * width]) * shrink).astype(BF16)
        val = dot(normed, wqkv[:, 2 * width :]).astype(BF16)
        for p in range(pairs):
            ks[p, wide(b)] = key[:, p * pw : (p + 1) * pw]
            vs[p, wide(b)] = val[:, p * pw : (p + 1) * pw]

        return 0

    loads["tok"].wait()
    loads["wqkv"].wait()
    lax.fori_loop(0, nw, keys_block, 0)

    def state_pair(p, _):
        for b in range(nb):
            feat = features_of(ks[p, block(b)], p)
            phk[p, block(b)] = feat
            end = ending(b)
            ve, vo = values_of(p, b)
            ue = dot_lt(jnp.where(end, ve, 0.0).astype(BF16), feat[:, :feat_n])
            uo = dot_lt(jnp.where(end, vo, 0.0).astype(BF16), feat[:, feat_n:])
            keep = keep_of(b)
            lst[b + 1, p, :pw] = keep * lst[b, p, :pw] + jnp.where(low_row, ue, uo)
            lst[b + 1, p, pw : pw + 8] = keep * lst[b, p, pw : pw + 8] + ue[hw : hw + 8]
            lst[b + 1, p, pw + 8 :] = keep * lst[b, p, pw + 8 :] + uo[:8]

        @pl.when(t == 0)
        def _():
            up_handle(p)


        @pl.when(p == 1)
        def _():
            w_spread(1)

        return 0

    lax.fori_loop(0, pairs, state_pair, 0)

    def queries_block(b, _):
        up_slots(b, 0, nw)
        query = (dot(n1s[wide(b)], wqkv[:, :width]) * shrink).astype(BF16)
        for p in range(pairs):
            qs[p, wide(b)] = query[:, p * pw : (p + 1) * pw]

        @pl.when(b == 0)
        def _():
            for k in range(3, tn):
                wz_copy(k).start()

        return 0

    lax.fori_loop(0, nw, queries_block, 0)

    def features_pair(p, _):
        up_slots(nw + p, nw, nw + pairs)
        for b in range(nw):
            phq[p, wide(b)] = features_of(qs[p, wide(b)], p)
        return 0

    lax.fori_loop(0, pairs, features_pair, 0)

    def state_halves(state):
        top = state[:pw]
        even = jnp.where(low_row, top, jnp.broadcast_to(state[pw : pw + 1], top.shape)).astype(BF16)
        odd = jnp.where(low_row, jnp.broadcast_to(state[pw + 8 : pw + 9], top.shape), top).astype(BF16)
        return even, odd

    slot = nw + pairs

    def inside_half(i, _):
        up_slots(slot + i, slot, slot + 2 * pairs)
        p, half = lax.div(i, 2), lax.rem(i, 2)

        @pl.when(i == 2)
        def _():
            w_swap(1)

        @pl.when(i == 6)
        def _():
            w_spread(2)

        for c in range(nb // 2):
            b = half * (nb // 2) + c
            for o, (val, part) in enumerate(zip(values_of(p, b), (facc, xh2))):
                fq = phq[p, block(b), o * feat_n : (o + 1) * feat_n]
                fk = phk[p, block(b), o * feat_n : (o + 1) * feat_n]
                scores = jnp.where(mask[b].astype(F32) > 0, dot_rt(fq, fk), 0.0).astype(BF16)
                part[block(b), lanes(p)] = dot(scores, val.astype(BF16))
        return 0

    lax.fori_loop(0, 2 * pairs, inside_half, 0)

    def attend_pair(p, _):
        up_slots(slot + 2 * pairs + p, slot + 2 * pairs, slot + 3 * pairs)

        @pl.when(t == tn - 1)
        def _():
            up_copy(p).wait_recv()

        incoming = chf_in[p].astype(F32)
        for b in range(nb):
            first_pass = jnp.where(before == prev_of(b), 1.0, 0.0)
            state = (lst[b, p] + first_pass * incoming).astype(BF16)
            sb[b, p] = state
            reach = reached(b)
            outs = []
            for o, (st, part) in enumerate(zip(state_halves(state.astype(F32)), (facc, xh2))):
                fq = phq[p, block(b), o * feat_n : (o + 1) * feat_n]
                outs.append(part[block(b), lanes(p)] + jnp.where(reach, dot_rt(fq, st), 0.0))
            inverse = 1.0 / jnp.where(low_lane, outs[1], outs[0])
            rsw_s[block(b), lanes(p)] = inverse
            num = jnp.where(low_lane, outs[0], outs[1])
            attn[block(b), lanes(p)] = (num * pltpu.roll(inverse, hw, 1)).astype(BF16)
        return 0

    lax.fori_loop(0, pairs, attend_pair, 0)

    def hidden_block(b, _):
        h1 = tok[wide(b)].astype(F32) + (dot(attn[wide(b)], wout[...]) + biases[0:1])
        scaled, inverse = normalized(h1)
        xh2[wide(b)] = scaled
        rstd2[wide(b)] = inverse
        n2s[wide(b)] = (scaled * g2[...]).astype(BF16)
        facc[wide(b)] = h1 + biases[2:3]
        return 0

    loads["wout"].wait()
    lax.fori_loop(0, nw, hidden_block, 0)
    loads["cot"].wait()

    def feed_chunk(s, _):
        @pl.when(s > 0)
        def _():
            for k in range(1, tn):

                @pl.when(s == k)
                def _(k=k):
                    wc_copy(k).wait_send()
                    wc_recv(k).wait_recv()
                    bz_copy(k).wait()

        def rows_block(b, total):
            w_in = wfull[s, 0]
            w_dn = wfull[s, 1]
            u = dot(n2s[wide(b)], w_in) + bfull[s, 0:1]
            u2 = u * u
            th = jnp.tanh(u * (SQRT_2_OVER_PI + SQRT_2_OVER_PI * CUBIC * u2))
            half = 0.5 + 0.5 * th
            act = (u * half).astype(BF16)
            slope = half + (0.5 * u) * (1.0 - th * th) * (
                SQRT_2_OVER_PI + 3.0 * SQRT_2_OVER_PI * CUBIC * u2
            )
            ad[0, wide(b)] = act
            facc[wide(b)] += dot(act, w_dn)
            du = (slope * dot_rt(cot[wide(b)], w_dn)).astype(BF16)
            ad[1, wide(b)] = du
            back = dot_rt(du, w_in)

            @pl.when(s == 0)
            def _():
                igrad[wide(b)] = back

            @pl.when(s > 0)
            def _():
                igrad[wide(b)] += back

            @pl.when((s >= 1) & (b == 0))
            def _():
                a_finish(jnp.maximum(s - 1, 0))

            @pl.when((s == 0) & (b == 0))
            def _():
                w_swap(2)

            @pl.when((s == 0) & (b == nw - 1))
            def _():
                for k in range(3, tn):
                    w_spread(k)

            @pl.when((s == 2) & (b == nw - 1))
            def _():
                for k in range(3, tn):
                    w_swap(k)

            return total + jnp.sum(du.astype(F32), 0, keepdims=True)

        total = lax.fori_loop(0, nw, rows_block, jnp.zeros((1, wfull.shape[3]), F32))
        vec[pl.ds(4 + s, 1)] = total

        @pl.when(s >= 2)
        def _():
            b_finish(jnp.maximum(s - 2, 0))

        for k in range(1, tn - 2, 2):

            @pl.when(s == k + 2)
            def _(k=k):
                c_start(k)

        gbuf[s, 0] = dot_lt(n2s[...], ad[1]).astype(BF16)
        gbuf[s, 1] = dot_lt(cot[...], ad[0]).astype(BF16)
        a_start(s)
        return 0

    lax.fori_loop(0, tn, feed_chunk, 0)

    def norm_back(dn, gain, scaled, inverse):
        g = dn * gain
        inner = jnp.mean(g, -1, keepdims=True)
        cross = jnp.mean(g * scaled, -1, keepdims=True)
        return inverse * (g - inner - scaled * cross)

    lane_id = iota((BR, pw), 1)

    def branch_block(b, carry):
        gl2, gbo, gbd = carry
        layer_out[block(b)] = facc[block(b)].astype(BF16)
        dy = cot[block(b)].astype(F32)
        dn2 = igrad[block(b)]
        scaled = xh2[block(b)]
        dh1 = dy + norm_back(dn2, g2[...], scaled, rstd2[block(b)])
        igrad[block(b)] = dh1
        dob = dh1.astype(BF16)
        n2s[block(b)] = dob
        dattn = dot_rt(dob, wout[...])
        reach = reached(b)
        for p in range(pairs):
            da = dattn[:, p * pw : (p + 1) * pw]
            inverse = rsw_s[block(b), p * pw : (p + 1) * pw]
            dnum = da * pltpu.roll(inverse, hw, 1)
            prod = da * attn[block(b), p * pw : (p + 1) * pw].astype(F32)
            high = prod.astype(BF16)
            rest = (prod - high.astype(F32)).astype(BF16)
            dden = -dot(jnp.concatenate([high, rest], 1), bsw[...]) * inverse
            dhi = dden.astype(BF16).astype(F32)
            dlo = dden - dhi
            even = jnp.where(lane_id == hw, dhi, jnp.where(lane_id == hw + 1, dlo, 0.0))
            odd = jnp.where(lane_id == 0, dhi, jnp.where(lane_id == 1, dlo, 0.0))
            even = jnp.where(low_lane, dnum, even)
            odd = jnp.where(low_lane, odd, dnum)
            ad[0, block(b), p * pw : (p + 1) * pw] = even.astype(BF16)
            ad[1, block(b), p * pw : (p + 1) * pw] = odd.astype(BF16)
            ge = dot_lt(jnp.where(reach, even, 0.0).astype(BF16), phq[p, block(b), :feat_n])
            go = dot_lt(jnp.where(reach, odd, 0.0).astype(BF16), phq[p, block(b), feat_n:])
            lst[b, p, :pw] = jnp.where(low_row, ge, go)
            lst[b, p, pw : pw + 8] = jnp.broadcast_to(ge[hw : hw + 1] + ge[hw + 1 : hw + 2], (8, feat_n))
            lst[b, p, pw + 8 :] = jnp.broadcast_to(go[0:1] + go[1:2], (8, feat_n))

        @pl.when(b == 1)
        def _():
            a_finish(tn - 1)

        return (
            gl2 + jnp.sum(dn2 * scaled, 0, keepdims=True),
            gbo + jnp.sum(dob.astype(F32), 0, keepdims=True),
            gbd + jnp.sum(dy, 0, keepdims=True),
        )

    zero_row = jnp.zeros((1, width), F32)
    gl2, gbo, gbd = lax.fori_loop(0, nb, branch_block, (zero_row,) * 3)
    store_layer().start()
    vec[1:2] = gbo
    vec[2:3] = gl2
    vec[3:4] = gbd
    half_blocks = nb // 2

    def grad_at(j, b):
        if isinstance(b, int):
            return j, b // half_blocks, pl.ds((b % half_blocks) * BR, BR)
        rows = pl.ds(pl.multiple_of(lax.rem(b, half_blocks) * BR, BR), BR)
        return j, lax.div(b, half_blocks), rows

    half = rows_n // 2

    def weight_grad(ja, pa, jb, pb):
        total = 0.0
        for h in range(2):
            both = [wfull[j, h, :half, lanes(p)] for j, p in ((ja, pa), (jb, pb))]
            total = total + dot_lt(n1s[h * half : (h + 1) * half], jnp.concatenate(both, 1))
        return total

    def arg_back(darg, x, p):
        both = dot_rt(darg, featx[p, : 2 * pw])
        return (both[:, :pw] + (2.0 * x.astype(F32)) * both[:, pw:]) * shrink

    out_grad = dot_lt(attn[...], n2s[...])
    for i in range(2):
        k_a_start(i, out_grad[:, i * 2 * pw : (i + 1) * 2 * pw])

    def query_half(i, _):
        down_slots(i, 0, 2 * pairs)
        p, half = lax.div(i, 2), lax.rem(i, 2)
        for c in range(nb // 2):
            b = half * (nb // 2) + c
            se, so = state_halves(sb[b, p].astype(F32))
            reach = reached(b)
            ve, vo = values_of(p, b)
            dargs = []
            for o, (val, st) in enumerate(((ve, se), (vo, so))):
                dn = ad[o, block(b), lanes(p)]
                cdn = jnp.where(reach, dn.astype(F32), 0.0).astype(BF16)
                fq = phq[p, block(b), o * feat_n : (o + 1) * feat_n]
                fk = phk[p, block(b), o * feat_n : (o + 1) * feat_n]
                da = jnp.where(mask[b].astype(F32) > 0, dot_rt(dn, val.astype(BF16)), 0.0).astype(BF16)
                dfq = dot(da, fk) + dot(cdn, st)
                dargs.append((dfq * fq.astype(F32)).astype(BF16))
            wfull[grad_at(0, b) + (lanes(p),)] = arg_back(
                jnp.concatenate(dargs, 1), qs[p, block(b)], p
            ).astype(BF16)

        @pl.when(i == 1)
        def _():
            k_a_finish(0)
            k_a_finish(1)
            b_finish(tn - 2)

        @pl.when(i == 3)
        def _():
            k_a_start(2, weight_grad(0, 0, 0, 1))

        @pl.when(i == 5)
        def _():
            k_a_finish(2)
            b_finish(tn - 1)
            c_start(tn - 1)

        @pl.when(i == 7)
        def _():
            k_a_start(3, weight_grad(0, 2, 0, 3))
            s_b_finish(0)
            s_b_finish(1)

        return 0

    lax.fori_loop(0, 2 * pairs, query_half, 0)

    def key_pair(p, _):
        down_slots(2 * (pairs + p), 2 * pairs, 4 * pairs)

        @pl.when(t == 0)
        def _():
            down_copy(p).wait_recv()

        grad = chb_in[p].astype(F32)
        for b in range(nb - 1, -1, -1):
            top = grad[:pw]
            halves = []
            for o in range(2):
                dz = jnp.broadcast_to(grad[pw + 8 * o : pw + 8 * o + 1], top.shape)
                dz_hi = dz.astype(BF16).astype(F32)
                at = hw * (1 - o)
                filler = jnp.where(row_id == at, dz_hi, jnp.where(row_id == at + 1, dz - dz_hi, 0.0))
                halves.append(
                    (jnp.where(low_row, top, filler) if o == 0 else jnp.where(low_row, filler, top)).astype(BF16)
                )
            end = ending(b)
            ve, vo = values_of(p, b)
            dargs, dvs = [], []
            for o, (val, ds) in enumerate(((ve, halves[0]), (vo, halves[1]))):
                dn = ad[o, block(b), lanes(p)]
                fq = phq[p, block(b), o * feat_n : (o + 1) * feat_n]
                fk = phk[p, block(b), o * feat_n : (o + 1) * feat_n]
                at = jnp.where(maskt[b].astype(F32) > 0, dot_rt(fk, fq), 0.0).astype(BF16)
                dat = jnp.where(maskt[b].astype(F32) > 0, dot_rt(val.astype(BF16), dn), 0.0).astype(BF16)
                ev = jnp.where(end, val, 0.0).astype(BF16)
                dfk = dot(dat, fq) + dot(ev, ds)
                dargs.append((dfk * fk.astype(F32)).astype(BF16))
                dvs.append(dot(at, dn) + jnp.where(end, dot_rt(fk, ds), 0.0))
            wfull[grad_at(1, b) + (lanes(p),)] = arg_back(
                jnp.concatenate(dargs, 1), ks[p, block(b)], p
            ).astype(BF16)
            wfull[grad_at(2, b) + (lanes(p),)] = jnp.where(
                low_lane, dvs[0], dvs[1]
            ).astype(BF16)
            if b > 0:
                grad = keep_of(b) * grad + lst[b, p]

        k_a_start(4 + p, weight_grad(1, p, 2, p))

        @pl.when(p == 0)
        def _():
            k_a_finish(3)
            s_b_finish(2)
            for k in range(tn - 2, 0, -2):
                c_start(k)

        @pl.when(p >= 1)
        def _():
            k_a_finish(3 + p)

        @pl.when(p == 1)
        def _():
            s_middle(0)
            s_middle(1)
            s_b_finish(3)

        @pl.when(p == 2)
        def _():
            c_finish()
            s_middle(2)
            s_b_finish(4)

        @pl.when(p == 3)
        def _():
            s_c_finish(0)
            s_c_finish(1)
            s_middle(3)
            s_b_finish(5)

        return 0

    lax.fori_loop(0, pairs, key_pair, 0)

    @pl.when(t < tn - 1)
    def _():
        for p in range(pairs):
            up_copy(p).wait_send()

    @pl.when(t > 0)
    def _():
        for p in range(pairs):
            down_copy(p).wait_send()

    def input_block(b, gl1):
        dn1 = dot_rt(wfull[0, b, :WR], wqkv[:, :width])
        for j in range(1, 3):
            dn1 = dn1 + dot_rt(wfull[j, b, :WR], wqkv[:, j * width : (j + 1) * width])
        scaled, inverse = normalized(tok[wide(b)].astype(F32))
        igrad[wide(b)] += norm_back(dn1, g1[...], scaled, inverse)
        store_grad(b).start()

        @pl.when(b == 0)
        def _():
            k_a_finish(7)
            s_middle(4)
            s_c_finish(2)

        @pl.when(b == 1)
        def _():
            k_b_finish(6)
            d_finish()

        return gl1 + jnp.sum(dn1 * scaled, 0, keepdims=True)

    vec[0:1] = lax.fori_loop(0, nw, input_block, zero_row)
    va_copy = remote(vec, va, va_s, va_r, core_dev)
    va_copy.start()
    s_middle(5)
    s_c_finish(3)
    va_copy.wait()
    vb[0] = vec[...] + va[...]
    vb_copies = [remote(vb.at[0], vb.at[k], vb_s.at[k - 1], vb_r.at[k - 1], peer_dev(k)) for k in range(1, npeer)]
    for copy in vb_copies:
        copy.start()
    k_b_finish(7)
    k_d_finish(0)
    k_d_finish(1)
    k_d_finish(2)
    s_c_finish(4)
    for copy in vb_copies:
        copy.wait()
    total = vb[peers[0]]
    for j in range(1, npeer):
        total = total + vb[peers[j]]
    vc[0] = total
    vc_copies = [remote(vc.at[0], vc.at[k], vc_s.at[k - 1], vc_r.at[k - 1], z_dev(k)) for k in range(1, tn)]
    for copy in vc_copies:
        copy.start()
    s_c_finish(5)
    k_c_finish(6)
    k_d_finish(3)
    k_c_finish(7)
    k_d_finish(4)
    for copy in vc_copies:
        copy.wait()
    total = vc[zs[0]]
    for j in range(1, tn):
        total = total + vc[zs[j]]
    own = vc[0, 4:5]
    for k in range(1, tn):
        own = own + vc[k, 4 + k : 5 + k]
    vec_out[...] = total
    vec_out[4:5] = own
    k_d_finish(5)
    k_d_finish(6)
    e_finish()
    k_d_finish(7)
    for i in range(8):
        k_e_finish(i)
    store_layer().wait()
    for b in range(nw):
        store_grad(b).wait()


def finish_kernel(
    layer_in, igrad_in, fin_h, fink_h, vec, layer_out, igrad, gwq_h, gwo_h, gwi_h, gwd_h, gl1, gbo, gl2, gbi, gbd,
    layer_v, igrad_v, fin, fink, gwq, gwo, gwi, gwd, in_s, out_s,
):
    def move(i, src, dst, sems):
        copy = pltpu.make_async_copy(src, dst, sems.at[i])
        copy.start()
        return copy

    pairs = fink.shape[0] // 2
    width, pw = fink.shape[2:]
    kinds = ((fink_h, fink), (fin_h, fin), (layer_in, layer_v), (igrad_in, igrad_v))
    loads = [move(i, src, dst, in_s) for i, (src, dst) in enumerate(kinds)]
    for row, out in enumerate((gl1, gbo, gl2, gbd, gbi)):
        out[...] = vec[row : row + 1]
    loads[0].wait()
    for p in range(pairs):
        at = slice(p * pw, (p + 1) * pw)
        gwq[:, at] = fink[2 + p // 2, p % 2].astype(F32)
        gwq[:, width + p * pw : width + (p + 1) * pw] = fink[4 + p, 0].astype(F32)
        gwq[:, 2 * width + p * pw : 2 * width + (p + 1) * pw] = fink[4 + p, 1].astype(F32)
    stores = [move(0, gwq, gwq_h, out_s)]
    for p in range(pairs):
        gwo[:, p * pw : (p + 1) * pw] = fink[p // 2, p % 2].astype(F32)
    stores.append(move(1, gwo, gwo_h, out_s))
    loads[2].wait()
    stores.append(move(2, layer_v, layer_out, out_s))
    loads[3].wait()
    stores.append(move(3, igrad_v, igrad, out_s))
    loads[1].wait()
    gwi[...] = fin[0].astype(F32)
    stores.append(move(4, gwi, gwi_h, out_s))
    gwd[...] = fin[1].astype(F32).T
    stores.append(move(5, gwd, gwd_h, out_s))
    for copy in stores:
        copy.wait()


def local(
    tn,
    dpn,
    tokens,
    cotangent,
    seq_lengths,
    features,
    ln1_gain,
    w_qkv,
    w_out,
    b_out,
    ln2_gain,
    w_in,
    b_in,
    w_down,
    b_down,
):
    rows_n, width = tokens.shape
    heads, hw, feat_n = features.shape
    pairs, pw, nb = heads // 2, 2 * hw, rows_n // BR
    ffl = w_in.shape[1]
    npeer = dpn // 2
    rp = width // npeer
    vrows = -(-(4 + tn) // 8) * 8
    dma = pltpu.SemaphoreType.DMA
    vmem = pl.BlockSpec(memory_space=pltpu.VMEM)
    anywhere = pl.BlockSpec(memory_space=pl.ANY)

    def scratch(shape, dtype=BF16):
        return pltpu.VMEM(shape, dtype)

    out = pl.pallas_call(
        functools.partial(layer_kernel, tn, dpn),
        out_shape=(
            jax.ShapeDtypeStruct((rows_n, width), BF16),
            jax.ShapeDtypeStruct((rows_n, width), F32),
            jax.ShapeDtypeStruct((2, width, width), BF16),
            jax.ShapeDtypeStruct((8, 2, width, pw), BF16),
            jax.ShapeDtypeStruct((vrows, width), F32),
        ),
        in_specs=[pl.BlockSpec(memory_space=pltpu.SMEM)]
        + [anywhere, anywhere, anywhere, vmem, anywhere, anywhere, vmem, vmem, anywhere, anywhere],
        out_specs=(anywhere, anywhere, vmem, vmem, vmem),
        scratch_shapes=[
            scratch((rows_n, width)),
            scratch((rows_n, width)),
            scratch((heads, hw, feat_n)),
            scratch((width, 3 * width)),
            scratch((width, width)),
            scratch((rows_n, width)),
            scratch((rows_n, width), F32),
            scratch((tn, 2, width, ffl)),
            scratch((tn, 8, ffl), F32),
            scratch((rows_n, width)),
            scratch((pairs, rows_n, pw)),
            scratch((pairs, rows_n, pw)),
            scratch((pairs, rows_n, pw)),
            scratch((pairs, rows_n, 2 * feat_n)),
            scratch((pairs, rows_n, 2 * feat_n)),
            scratch((pairs, 3 * pw, 2 * feat_n)),
            scratch((2 * pw, pw)),
            scratch((nb, BR, BR)),
            scratch((nb, BR, BR)),
            scratch((nb + 1, pairs, pw + 16, feat_n), F32),
            scratch((nb, pairs, pw + 16, feat_n)),
            scratch((rows_n, width), F32),
            scratch((rows_n, width)),
            scratch((rows_n, width), F32),
            scratch((rows_n, width), F32),
            scratch((rows_n, 1), F32),
            scratch((rows_n, width)),
            scratch((2, rows_n, width)),
            scratch((pairs, pw + 16, feat_n)),
            scratch((pairs, pw + 16, feat_n)),
            scratch((pairs, pw + 16, feat_n)),
            scratch((pairs, pw + 16, feat_n)),
            scratch((tn, 2, width, width)),
            scratch((2, width, width)),
            scratch((4, npeer - 1, rp, width)),
            scratch((tn - 1, rp, width)),
            scratch((8, 2, width, pw)),
            scratch((4, width, pw)),
            scratch((8, npeer - 1, rp, pw)),
            scratch((8, max(tn, 2 * (tn - 1).bit_length()), rp, pw)),
            scratch((vrows, width), F32),
            scratch((vrows, width), F32),
            scratch((npeer, vrows, width), F32),
            scratch((tn, vrows, width), F32),
            dma((7,)),
            dma((1 + rows_n // WR,)),
            dma((tn - 1,)),
            dma((tn - 1,)),
            dma((tn - 1,)),
            dma((tn - 1,)),
            dma((tn - 1, npeer - 1)),
            dma((tn - 1, npeer - 1)),
            dma((tn - 1,)),
            dma((tn - 1,)),
            dma((pairs,)),
            dma((pairs,)),
            dma((pairs,)),
            dma((pairs,)),
            dma((tn,)),
            dma((tn,)),
            dma((tn, npeer - 1)),
            dma((tn, npeer - 1)),
            dma((tn - 1,)),
            dma((tn - 1,)),
            dma((npeer - 1,)),
            dma((npeer - 1,)),
            dma(()),
            dma(()),
            dma((8,)),
            dma((8,)),
            dma((8, npeer - 1)),
            dma((8, npeer - 1)),
            dma((8, tn - 1)),
            dma((8, tn - 1)),
            dma((8, npeer - 1)),
            dma((8, npeer - 1)),
            dma((8,)),
            dma((8,)),
            dma(()),
            dma(()),
            dma((npeer - 1,)),
            dma((npeer - 1,)),
            dma((tn - 1,)),
            dma((tn - 1,)),
        ],
        compiler_params=pltpu.CompilerParams(
            collective_id=0, has_side_effects=True, vmem_limit_bytes=63 * 1024 * 1024
        ),
    )(
        seq_lengths,
        tokens,
        cotangent,
        features,
        ln1_gain[None],
        w_qkv,
        w_out,
        jnp.stack([b_out, b_in, b_down]).astype(F32),
        ln2_gain[None],
        w_in,
        w_down,
    )
    row = jax.ShapeDtypeStruct((1, width), F32)

    def square(n):
        return jax.ShapeDtypeStruct((width, n * width), F32)

    done = pl.pallas_call(
        finish_kernel,
        out_shape=(out[0], out[1], square(3), square(1), square(1), square(1)) + (row,) * 5,
        in_specs=[anywhere] * 4 + [vmem],
        out_specs=(anywhere,) * 6 + (vmem,) * 5,
        scratch_shapes=[
            scratch((rows_n, width)),
            scratch((rows_n, width), F32),
            scratch((2, width, width)),
            scratch((8, 2, width, pw)),
            scratch((width, 3 * width), F32),
            scratch((width, width), F32),
            scratch((width, width), F32),
            scratch((width, width), F32),
            dma((4,)),
            dma((6,)),
        ],
        compiler_params=pltpu.CompilerParams(vmem_limit_bytes=63 * 1024 * 1024),
    )(*out)
    layer_out, input_grad, gwq, gwo, gwi, gwd, gl1, gbo, gl2, gbi, gbd = done
    return (
        layer_out,
        input_grad,
        gl1[0],
        gwq,
        gwo,
        gbo[0],
        gl2[0],
        gwi,
        gbi[0],
        gwd,
        gbd[0],
    )


def solution(mesh):
    tn, dpn = mesh.shape["tensor"], mesh.shape["dp"]
    rows = P(("dp", "tensor"), None)
    return jax.shard_map(
        functools.partial(local, tn, dpn),
        mesh=mesh,
        in_specs=(
            rows,
            rows,
            P("dp", None),
            P(),
            P(),
            P(),
            P(),
            P(),
            P(),
            P(None, "tensor"),
            P("tensor"),
            P("tensor", None),
            P(),
        ),
        out_specs=(
            rows,
            rows,
            P(),
            P(),
            P(),
            P(),
            P(),
            P(None, "tensor"),
            P("tensor"),
            P("tensor", None),
            P(),
        ),
        check_vma=False,
    )
```

time: 187 us -> 127 us (0.68)
  Pallas kernels: 168 us -> 123 us
  other arithmetic: 8.51 us -> 0.61 us
  local copies, waits for them, and re-layouts: 8.35 us -> 2.05 us
    pallas_call x1, Pallas kernels: 168 us -> 116 us  [local(): pl.pallas_call(functools.partial(layer_kernel, tn, dpn), out_shape=(jax.S...]
    pallas_call x0 -> x1, Pallas kernels: none -> 7.03 us  [local(): pl.pallas_call(finish_kernel, out_shape=(out[0], out[1], square(3), squar...]
    unnamed x7 -> x0, local copies, waits for them, and re-layouts: 3.6 us -> none
    concatenate x1 -> x0, other arithmetic: 3.24 us -> none  [local(): jnp.concatenate([fin[1, 1], fin[2, 0], fin[2, 1]], 1)]
    broadcast_in_dim x2 -> x0, other arithmetic: 2.52 us -> none  [the longest x1 1.26 us: local(): b_out.astype(F32)[None]]
    convert_element_type x1, other arithmetic: 2.75 us -> 0.61 us  [local(): jnp.stack([b_out, b_in, b_down]).astype(F32)]
    another operation x0 -> x3, local copies, waits for them, and re-layouts: none -> 2.05 us  [local(): jnp.stack([b_out, b_in, b_down]).astype(F32)]
    transpose x1 -> x0, local copies, waits for them, and re-layouts: 1.99 us -> none  [local(): fin[0, 1]]
where the time goes in v2:
time: 127 us
  Pallas kernels  123 us (97%)
  local copies, waits for them, and re-layouts  2.05 us (2%)
    pallas_call x1, Pallas kernels, local(): pl.pallas_call(functools.partial(layer_kernel, tn, dpn), out_shape=(jax.S...  116 us
    pallas_call x1, Pallas kernels, local(): pl.pallas_call(finish_kernel, out_shape=(out[0], out[1], square(3), squar...  7.03 us

profile of v2, /device:TPU:0, one launch (start us, length us, event | category | flops | bytes accessed | tf_op | source)
XLA Modules:
  0.0 126.5 jit_solution(2334469124286390418)
XLA Ops:
  0.6 0.7 stack.12
  1.3 0.7 stack.13
  2.0 0.7 stack.14
  2.7 0.6 maximum_convert_fusion.biases
  3.3 116.0 %shard_map.212 = (bf16[1024,512]{1,0:T(8,128)(2,1)}, f32[1024,512]{1,0:T(8,128)}, bf16[2,512,512]{2,1,0:T(8,128)(2,1)}, bf16[8,2,512,128]{3,2,1,0:T(8,128)(2,1)}, f32[8,512]{1,0:T(8,128)}) custom-call(s32[1,2]{1,0:T(1,128)} %lens.1, bf16[1024,512]{1,0:T(8,128)(2,1)} %tok_h.1, bf16[1024,512]{1,0:T(8,128)(2,1)} %cot_h.1, bf16[8,64,256]{2,1,0:T(8,128)(2,1)} %feats_h.1, ...), custom_call_target="tpu_custom_call" | custom-call | tf_op jit(solution)/shard_map/pallas_call | solution.py:1157
  119.3 7.0 %shard_map.213 = (bf16[1024,512]{1,0:T(8,128)(2,1)}, f32[1024,512]{1,0:T(8,128)}, f32[512,1536]{1,0:T(8,128)}, f32[512,512]{1,0:T(8,128)}, f32[512,512]{1,0:T(8,...) custom-call(bf16[1024,512]{1,0:T(8,128)(2,1)} %get-tuple-element.27., ...), custom_call_target="tpu_custom_call" | custom-call | tf_op jit(solution)/shard_map/pallas_call | solution.py:1276

commit v3 on v2

--- a/solution.py
+++ b/solution.py
@@ -48,24 +48,28 @@
     tok_h,
     cot_h,
     feats_h,
-    g1,
+    g1_h,
     wqkv_h,
     wout_h,
-    biases,
-    g2,
+    biases_h,
+    g2_h,
     win_h,
     wdn_h,
     layer_h,
     igrad_h,
+    fin_h,
+    fink_h,
+    vec_out,
     fin,
     fink,
-    vec_out,
+    g1,
+    g2,
+    biases,
     tok,
     cot,
     feats,
     wqkv,
     wout,
-    layer_out,
     igrad,
     wfull,
     bfull,
@@ -76,6 +80,7 @@
     phq,
     phk,
     featx,
+    norms,
     bsw,
     mask,
     maskt,
@@ -182,24 +187,36 @@
     def load(i, src, dst):
         return pltpu.make_async_copy(src, dst, in_s.at[i])
 
-    loads = {
-        "win": load(0, win_h, wfull.at[0, 0]),
-        "wdn": load(1, wdn_h, wfull.at[0, 1]),
-        "tok": load(2, tok_h, tok),
-        "wqkv": load(3, wqkv_h, wqkv),
-        "feats": load(4, feats_h, feats),
-        "wout": load(5, wout_h, wout),
-        "cot": load(6, cot_h, cot),
+    pairs_in = {
+        "feats": (feats_h, feats),
+        "g1": (g1_h, g1),
+        "g2": (g2_h, g2),
+        "biases": (biases_h, biases),
+        "win": (win_h, wfull.at[0, 0]),
+        "wdn": (wdn_h, wfull.at[0, 1]),
+        "tok": (tok_h, tok),
+        "wqkv": (wqkv_h, wqkv),
+        "wout": (wout_h, wout),
+        "cot": (cot_h, cot),
     }
+    loads = {name: load(i, *pair) for i, (name, pair) in enumerate(pairs_in.items())}
     for copy in loads.values():
         copy.start()
 
     def store_layer():
-        return pltpu.make_async_copy(layer_out, layer_h, out_s.at[0])
+        half = layer_h.shape[0] // 2
+        for h in range(2):
+            pltpu.make_async_copy(wfull.at[tn - 1, h], layer_h.at[pl.ds(h * half, half)], out_s.at[0]).start()
 
     def store_grad(b):
         rows = pl.ds(pl.multiple_of(b * WR, WR), WR)
-        return pltpu.make_async_copy(igrad.at[rows], igrad_h.at[rows], out_s.at[1 + b])
+        pltpu.make_async_copy(igrad.at[rows], igrad_h.at[rows], out_s.at[1]).start()
+
+    def store_fin():
+        return pltpu.make_async_copy(fin, fin_h, out_s.at[2])
+
+    def store_fink(i):
+        return pltpu.make_async_copy(fink.at[i], fink_h.at[i], out_s.at[3])
 
     bar = pltpu.get_barrier_semaphore()
     targets = [core_dev] + [peer_dev(k) for k in range(1, npeer)] + [z_dev(k) for k in range(1, tn)]
@@ -211,52 +228,55 @@
             src_ref=src, dst_ref=dst, send_sem=ss, recv_sem=rs, device_id=dev, device_id_type=MESH
         )
 
+    def arrived(ref, sem):
+        remote(ref, ref, a_s, sem, core_dev).wait_recv()
+
+    def sent(ref, sem):
+        remote(ref, ref, sem, a_r.at[0], core_dev).wait_send()
+
     def bz_copy(k):
-        return remote(bfull.at[0], bfull.at[k], bz_s.at[k - 1], bz_r.at[k - 1], z_dev(k))
+        return remote(bfull.at[0], bfull.at[k], bz_s, bz_r, z_dev(k))
 
     def wz_copy(k):
+        source, via = (0, k) if k == 1 or k % 2 == 0 else (k - 1, 1)
         return remote(
-            wfull.at[0, cb, own_rows()], wfull.at[k, cb, own_rows()], wz_s.at[k - 1], wz_r.at[k - 1], z_dev(k)
+            wfull.at[source, cb, own_rows()], wfull.at[k, cb, own_rows()], wz_s, wz_r.at[k - 1], z_dev(via)
         )
 
     def wx_copy(k, j):
         here = wfull.at[k, cb, own_rows()]
-        return remote(here, here, wx_s.at[k - 1, j - 1], wx_r.at[k - 1, j - 1], peer_dev(j))
-
-    def wx_recv(k, j):
-        here = wfull.at[k, cb, peer_rows(j)]
-        return remote(here, here, wx_s.at[k - 1, j - 1], wx_r.at[k - 1, j - 1], peer_dev(j))
+        return remote(here, here, wx_s, wx_r.at[k - 1], peer_dev(j))
 
     def wc_copy(k):
-        return remote(wfull.at[k, cb], wfull.at[k, cb], wc_s.at[k - 1], wc_r.at[k - 1], core_dev)
+        return remote(wfull.at[k, cb], wfull.at[k, cb], wc_s, wc_r.at[k - 1], core_dev)
 
     def wc_recv(k):
         here = wfull.at[k, 1 - cb]
-        return remote(here, here, wc_s.at[k - 1], wc_r.at[k - 1], core_dev)
+        return remote(here, here, wc_s, wc_r.at[k - 1], core_dev)
 
     def w_spread(k):
-        wz_copy(k).wait()
+        wz_copy(k).wait_recv()
+        if k > 1 and k % 2 == 0:
+            wz_copy(k + 1).start()
         for j in range(1, npeer):
             wx_copy(k, j).start()
 
     def w_swap(k):
-        for j in range(1, npeer):
-            wx_copy(k, j).wait_send()
-            wx_recv(k, j).wait_recv()
+        arrived(wfull.at[k, cb, pl.ds(0, (npeer - 1) * rp)], wx_r.at[k - 1])
         wc_copy(k).start()
 
     levels = (tn - 1).bit_length()
-    up_first = (1, 3, 5, 8), (9, 11, 14, 16)
+    up_first = (1, 3, 5, 7), (8, 9, 10, 12)
 
     def up_due(at, p):
-        return up_first[at - 1][p % 4] if at < 3 and p < 4 else 14 + p
+        return up_first[at - 1][p % 4] if at < 3 and p < 4 else 10 + p
 
     def down_due(hops, p):
         due = min(3 * hops + p, 8 + 2 * p)
         return due + due % 2 if due > 8 else due
 
     def up_copy(p):
-        return remote(chf_out.at[p], chf_in.at[p], chf_s.at[p], chf_r.at[p], (dp, lax.rem(t + 1, tn)))
+        return remote(chf_out.at[p], chf_in.at[p], chf_s, chf_r.at[p], (dp, lax.rem(t + 1, tn)))
 
     def up_handle(p):
         @pl.when(t > 0)
@@ -276,7 +296,7 @@
                         up_handle(p)
 
     def down_copy(p):
-        return remote(chb_out.at[p], chb_in.at[p], chb_s.at[p], chb_r.at[p], (dp, lax.rem(t + tn - 1, tn)))
+        return remote(chb_out.at[p], chb_in.at[p], chb_s, chb_r.at[p], (dp, lax.rem(t + tn - 1, tn)))
 
     def down_handle(p):
         @pl.when(t < tn - 1)
@@ -298,24 +318,25 @@
                     def _(p=p):
                         down_handle(p)
 
-    def a_copy(s):
-        s = jnp.int32(s)
-        return remote(gbuf.at[s, 1 - cb], ra.at[lax.rem(s, 2)], a_s.at[s], a_r.at[s], core_dev)
+    def place_of(turn):
+        return jnp.where(turn < tn // 2, 2 * turn + 1, 2 * (tn - 1 - turn))
+
+    def a_copy(turn):
+        turn = jnp.int32(turn)
+        return remote(
+            gbuf.at[place_of(turn), 1 - cb], ra.at[lax.rem(turn, 2)], a_s, a_r.at[lax.rem(turn, 2)], core_dev
+        )
 
     def b_copy(s, k):
         s = jnp.int32(s)
-        return remote(gbuf.at[s, cb, peer_rows(k)], rb.at[lax.rem(s, 4), k - 1], b_s.at[s, k - 1], b_r.at[s, k - 1], peer_dev(k))
+        return remote(gbuf.at[s, cb, peer_rows(k)], rb.at[lax.rem(s, 4), k - 1], b_s, b_r.at[s], peer_dev(k))
 
     def c_copy(s):
-        return remote(gbuf.at[s, cb, own_rows()], rc.at[s - 1], c_s.at[s - 1], c_r.at[s - 1], z_dev(s & -s))
+        return remote(gbuf.at[s, cb, own_rows()], rc.at[s - 1], c_s, c_r.at[s - 1], z_dev(s & -s))
 
     def d_copy(k):
         here = fin.at[cb, own_rows()]
-        return remote(here, here, d_s.at[k - 1], d_r.at[k - 1], peer_dev(k))
-
-    def d_recv(k):
-        here = fin.at[cb, peer_rows(k)]
-        return remote(here, here, d_s.at[k - 1], d_r.at[k - 1], peer_dev(k))
+        return remote(here, here, d_s, d_r, peer_dev(k))
 
     def e_copy():
         return remote(fin.at[cb], fin.at[cb], e_s, e_r, core_dev)
@@ -325,49 +346,45 @@
 
     def ka_copy(i):
         i = jnp.int32(i)
-        return remote(kbuf.at[i, 1 - cb], kra.at[lax.rem(i, 4)], ka_s.at[i], ka_r.at[i], core_dev)
+        return remote(kbuf.at[i, 1 - cb], kra.at[lax.rem(i, 4)], ka_s, ka_r.at[lax.rem(i, 4)], core_dev)
 
     def kb_copy(i, k):
         return remote(
-            kbuf.at[i, cb, peer_rows(k)], krb.at[i, k - 1], kb_s.at[i, k - 1], kb_r.at[i, k - 1], peer_dev(k)
+            kbuf.at[i, cb, peer_rows(k)], krb.at[i, k - 1], kb_s, kb_r.at[i], peer_dev(k)
         )
 
     def kc_copy(i, k):
-        return remote(krc.at[i, 0], krc.at[i, k], kc_s.at[i, k - 1], kc_r.at[i, k - 1], z_dev(k))
+        return remote(krc.at[i, 0], krc.at[i, k], kc_s.at[0], kc_r.at[i, 0], z_dev(k))
 
     def ks_copy(i, l):
         return remote(
-            krc.at[i, 2 * l], krc.at[i, 2 * l + 1], kc_s.at[i, l], kc_r.at[i, l], z_dev(1 << l)
+            krc.at[i, 2 * l], krc.at[i, 2 * l + 1], kc_s.at[1], kc_r.at[i, l], z_dev(1 << l)
         )
 
     def kd_copy(i, k):
         here = fink.at[i, cb, own_rows()]
-        return remote(here, here, kd_s.at[i, k - 1], kd_r.at[i, k - 1], peer_dev(k))
-
-    def kd_recv(i, k):
-        here = fink.at[i, cb, peer_rows(k)]
-        return remote(here, here, kd_s.at[i, k - 1], kd_r.at[i, k - 1], peer_dev(k))
+        return remote(here, here, kd_s, kd_r.at[i], peer_dev(k))
 
     def ke_copy(i):
-        return remote(fink.at[i, cb], fink.at[i, cb], ke_s.at[i], ke_r.at[i], core_dev)
+        return remote(fink.at[i, cb], fink.at[i, cb], ke_s, ke_r.at[i], core_dev)
 
     def ke_recv(i):
-        return remote(fink.at[i, 1 - cb], fink.at[i, 1 - cb], ke_s.at[i], ke_r.at[i], core_dev)
-
-    def a_start(s):
-        a_copy(s).start()
-
-    def a_finish(s):
-        s = jnp.int32(s)
-        a_copy(s).wait()
-        gbuf[s, cb] = (gbuf[s, cb].astype(F32) + ra[lax.rem(s, 2)].astype(F32)).astype(BF16)
+        return remote(fink.at[i, 1 - cb], fink.at[i, 1 - cb], ke_s, ke_r.at[i], core_dev)
+
+    def a_start(turn):
+        a_copy(turn).start()
+
+    def a_finish(turn):
+        turn = jnp.int32(turn)
+        a_copy(turn).wait_recv()
+        s = place_of(turn)
+        gbuf[s, cb] = (gbuf[s, cb].astype(F32) + ra[lax.rem(turn, 2)].astype(F32)).astype(BF16)
         for k in range(1, npeer):
             b_copy(s, k).start()
 
     def b_sum(s):
         s = jnp.int32(s)
-        for k in range(1, npeer):
-            b_copy(s, k).wait()
+        arrived(rb.at[lax.rem(s, 4)], b_r.at[s])
         total = gbuf[s, cb, own_rows()].astype(F32)
         for k in range(1, npeer):
             total = total + rb[lax.rem(s, 4), k - 1].astype(F32)
@@ -379,7 +396,7 @@
     def c_add(s):
         step = 1
         while step < (s & -s if s else tn):
-            c_copy(s + step).wait()
+            c_copy(s + step).wait_recv()
             gbuf[s, cb, own_rows()] = (
                 gbuf[s, cb, own_rows()].astype(F32) + rc[s + step - 1].astype(F32)
             ).astype(BF16)
@@ -393,7 +410,7 @@
         total = gbuf[0, cb, own_rows()].astype(F32)
         step = 1
         while step < tn:
-            c_copy(step).wait()
+            c_copy(step).wait_recv()
             total = total + rc[step - 1].astype(F32)
             step *= 2
         fin[cb, own_rows()] = total.astype(BF16)
@@ -401,13 +418,10 @@
             d_copy(k).start()
 
     def d_finish():
-        for k in range(1, npeer):
-            d_copy(k).wait_send()
-            d_recv(k).wait_recv()
+        arrived(fin.at[0, pl.ds(0, (npeer - 1) * rp)], d_r)
         e_copy().start()
 
     def e_finish():
-        e_copy().wait_send()
         e_recv().wait_recv()
 
     def k_a_start(i, both):
@@ -417,14 +431,13 @@
 
     def k_a_finish(i):
         i = jnp.int32(i)
-        ka_copy(i).wait()
+        ka_copy(i).wait_recv()
         kbuf[i, cb] = (kbuf[i, cb].astype(F32) + kra[lax.rem(i, 4)].astype(F32)).astype(BF16)
         for k in range(1, npeer):
             kb_copy(i, k).start()
 
     def k_b_sum(i):
-        for k in range(1, npeer):
-            kb_copy(i, k).wait()
+        arrived(krb.at[i], kb_r.at[i])
         total = kbuf[i, cb, own_rows()].astype(F32)
         for k in range(1, npeer):
             total = total + krb[i, k - 1].astype(F32)
@@ -441,8 +454,7 @@
             kc_copy(i, k).start()
 
     def k_c_finish(i):
-        for k in range(1, tn):
-            kc_copy(i, k).wait()
+        arrived(krc.at[i, pl.ds(1, tn - 1)], kc_r.at[i, 0])
         total = krc[i, zs[0]].astype(F32)
         for j in range(1, tn):
             total = total + krc[i, zs[j]].astype(F32)
@@ -453,7 +465,7 @@
         ks_copy(i, 0).start()
 
     def s_sum(i, l):
-        ks_copy(i, l).wait()
+        ks_copy(i, l).wait_recv()
         return krc[i, 2 * l].astype(F32) + krc[i, 2 * l + 1].astype(F32)
 
     def s_middle(i):
@@ -465,13 +477,10 @@
         k_spread(i, s_sum(i, levels - 1))
 
     def k_d_finish(i):
-        for k in range(1, npeer):
-            kd_copy(i, k).wait_send()
-            kd_recv(i, k).wait_recv()
+        arrived(fink.at[i, 0, pl.ds(0, (npeer - 1) * rp)], kd_r.at[i])
         ke_copy(i).start()
 
     def k_e_finish(i):
-        ke_copy(i).wait_send()
         ke_recv(i).wait_recv()
 
     offsets = [jnp.int32(0)]
@@ -526,16 +535,18 @@
     low_row = iota((pw, feat_n), 0) < hw
     row_id = iota((pw, feat_n), 0)
 
-    loads["feats"].wait()
+    for name in ("feats", "g1", "g2", "biases"):
+        loads[name].wait()
     featx[...] = jnp.zeros_like(featx)
     for p in range(pairs):
         for o in range(2):
             featx[p, o * hw : (o + 1) * hw, o * feat_n : (o + 1) * feat_n] = feats[2 * p + o]
-            for rep in (1, 2):
-                featx[
-                    p, rep * pw + o * hw : rep * pw + (o + 1) * hw, o * feat_n : (o + 1) * feat_n
-                ] = jnp.full((hw, feat_n), -0.5, BF16)
+            featx[p, pw + o * hw : pw + (o + 1) * hw, o * feat_n : (o + 1) * feat_n] = jnp.full(
+                (hw, feat_n), -0.5, BF16
+            )
     ri, ci = iota((2 * pw, pw), 0), iota((2 * pw, pw), 1)
+    ro, co = iota((2 * pw, 2 * pw), 0), iota((2 * pw, 2 * pw), 1)
+    norms[...] = jnp.where((lax.rem(ro, pw) < hw) == (co < pw), -0.5, 0.0).astype(BF16)
     swap = (lax.rem(ri, pw) < hw) != (ci < hw)
     bsw[...] = jnp.where(swap, 1.0, 0.0).astype(BF16)
 
@@ -563,7 +574,7 @@
     loads["win"].wait()
     loads["wdn"].wait()
     pl.semaphore_wait(bar, len(targets))
-    bfull[0] = jnp.broadcast_to(biases[1:2], bfull.shape[1:])
+    bfull[0] = jnp.broadcast_to(biases[:, width : width + bfull.shape[2]], bfull.shape[1:])
     for k in range(1, tn):
         bz_copy(k).start()
     wz_copy(1).start()
@@ -574,7 +585,9 @@
         square = wide * wide
         high = square.astype(BF16)
         rest = (square - high.astype(F32)).astype(BF16)
-        arg = dot(jnp.concatenate([x, high, rest], 1), featx[p])
+        norm = dot(jnp.concatenate([high, rest], 1), norms[...])
+        repeats = [norm[:, :pw]] * (feat_n // pw) + [norm[:, pw:]] * (feat_n // pw)
+        arg = dot(x, featx[p, :pw]) + jnp.concatenate(repeats, 1)
         return (jnp.exp(arg) * featscale).astype(BF16)
 
     def normalized(x):
@@ -604,9 +617,10 @@
     lax.fori_loop(0, nw, keys_block, 0)
 
     def state_pair(p, _):
+        for c in range(nw):
+            phk[p, wide(c)] = features_of(ks[p, wide(c)], p)
         for b in range(nb):
-            feat = features_of(ks[p, block(b)], p)
-            phk[p, block(b)] = feat
+            feat = phk[p, block(b)]
             end = ending(b)
             ve, vo = values_of(p, b)
             ue = dot_lt(jnp.where(end, ve, 0.0).astype(BF16), feat[:, :feat_n])
@@ -621,7 +635,7 @@
             up_handle(p)
 
 
-        @pl.when(p == 1)
+        @pl.when(p == 3)
         def _():
             w_spread(1)
 
@@ -635,10 +649,9 @@
         for p in range(pairs):
             qs[p, wide(b)] = query[:, p * pw : (p + 1) * pw]
 
-        @pl.when(b == 0)
-        def _():
-            for k in range(3, tn):
-                wz_copy(k).start()
+        @pl.when(b == nw - 1)
+        def _():
+            w_spread(2)
 
         return 0
 
@@ -660,20 +673,14 @@
 
     slot = nw + pairs
 
-    def inside_half(i, _):
-        up_slots(slot + i, slot, slot + 2 * pairs)
-        p, half = lax.div(i, 2), lax.rem(i, 2)
-
-        @pl.when(i == 2)
-        def _():
-            w_swap(1)
-
-        @pl.when(i == 6)
-        def _():
-            w_spread(2)
-
-        for c in range(nb // 2):
-            b = half * (nb // 2) + c
+    def inside_pair(p, _):
+        up_slots(slot + p, slot, slot + pairs)
+
+        @pl.when(p == 3)
+        def _():
+            w_spread(3)
+
+        for b in range(nb):
             for o, (val, part) in enumerate(zip(values_of(p, b), (facc, xh2))):
                 fq = phq[p, block(b), o * feat_n : (o + 1) * feat_n]
                 fk = phk[p, block(b), o * feat_n : (o + 1) * feat_n]
@@ -681,10 +688,14 @@
                 part[block(b), lanes(p)] = dot(scores, val.astype(BF16))
         return 0
 
-    lax.fori_loop(0, 2 * pairs, inside_half, 0)
+    lax.fori_loop(0, pairs, inside_pair, 0)
 
     def attend_pair(p, _):
-        up_slots(slot + 2 * pairs + p, slot + 2 * pairs, slot + 3 * pairs)
+        up_slots(slot + pairs + p, slot + pairs, slot + 2 * pairs)
+
+        @pl.when(p == 2)
+        def _():
+            w_swap(1)
 
         @pl.when(t == tn - 1)
         def _():
@@ -709,28 +720,28 @@
     lax.fori_loop(0, pairs, attend_pair, 0)
 
     def hidden_block(b, _):
-        h1 = tok[wide(b)].astype(F32) + (dot(attn[wide(b)], wout[...]) + biases[0:1])
+        h1 = tok[wide(b)].astype(F32) + (dot(attn[wide(b)], wout[...]) + biases[:, :width])
         scaled, inverse = normalized(h1)
         xh2[wide(b)] = scaled
         rstd2[wide(b)] = inverse
         n2s[wide(b)] = (scaled * g2[...]).astype(BF16)
-        facc[wide(b)] = h1 + biases[2:3]
+        facc[wide(b)] = h1 + biases[:, width + bfull.shape[2] :]
         return 0
 
     loads["wout"].wait()
     lax.fori_loop(0, nw, hidden_block, 0)
     loads["cot"].wait()
 
-    def feed_chunk(s, _):
+    def feed_chunk(turn, _):
+        s = place_of(turn)
+
         @pl.when(s > 0)
         def _():
             for k in range(1, tn):
 
                 @pl.when(s == k)
                 def _(k=k):
-                    wc_copy(k).wait_send()
                     wc_recv(k).wait_recv()
-                    bz_copy(k).wait()
 
         def rows_block(b, total):
             w_in = wfull[s, 0]
@@ -749,53 +760,47 @@
             ad[1, wide(b)] = du
             back = dot_rt(du, w_in)
 
-            @pl.when(s == 0)
+            @pl.when(turn == 0)
             def _():
                 igrad[wide(b)] = back
 
-            @pl.when(s > 0)
+            @pl.when(turn > 0)
             def _():
                 igrad[wide(b)] += back
 
-            @pl.when((s >= 1) & (b == 0))
+            @pl.when((turn >= 1) & (b == 0))
             def _():
-                a_finish(jnp.maximum(s - 1, 0))
-
-            @pl.when((s == 0) & (b == 0))
+                a_finish(jnp.maximum(turn - 1, 0))
+
+            @pl.when((turn == 0) & (b == 0))
             def _():
                 w_swap(2)
 
-            @pl.when((s == 0) & (b == nw - 1))
+            @pl.when((turn == 0) & (b == nw - 1))
             def _():
-                for k in range(3, tn):
-                    w_spread(k)
-
-            @pl.when((s == 2) & (b == nw - 1))
-            def _():
-                for k in range(3, tn):
-                    w_swap(k)
+                w_swap(3)
 
             return total + jnp.sum(du.astype(F32), 0, keepdims=True)
 
         total = lax.fori_loop(0, nw, rows_block, jnp.zeros((1, wfull.shape[3]), F32))
         vec[pl.ds(4 + s, 1)] = total
 
-        @pl.when(s >= 2)
-        def _():
-            b_finish(jnp.maximum(s - 2, 0))
-
-        for k in range(1, tn - 2, 2):
-
-            @pl.when(s == k + 2)
-            def _(k=k):
-                c_start(k)
+        @pl.when(turn == tn - 1)
+        def _():
+            b_finish(1)
+            c_start(1)
 
         gbuf[s, 0] = dot_lt(n2s[...], ad[1]).astype(BF16)
         gbuf[s, 1] = dot_lt(cot[...], ad[0]).astype(BF16)
-        a_start(s)
+        a_start(turn)
         return 0
 
+    arrived(bfull.at[pl.ds(1, tn - 1)], bz_r)
     lax.fori_loop(0, tn, feed_chunk, 0)
+    sent(bfull.at[pl.ds(1, tn - 1)], bz_s)
+    sent(wfull.at[pl.ds(0, tn - 1), 0, pl.ds(0, rp)], wz_s)
+    sent(wfull.at[pl.ds(0, tn - 1), 0, pl.ds(0, (npeer - 1) * rp)], wx_s)
+    sent(wfull.at[pl.ds(0, tn - 1), 0], wc_s)
 
     def norm_back(dn, gain, scaled, inverse):
         g = dn * gain
@@ -803,25 +808,25 @@
         cross = jnp.mean(g * scaled, -1, keepdims=True)
         return inverse * (g - inner - scaled * cross)
 
-    lane_id = iota((BR, pw), 1)
 
     def branch_block(b, carry):
         gl2, gbo, gbd = carry
-        layer_out[block(b)] = facc[block(b)].astype(BF16)
-        dy = cot[block(b)].astype(F32)
-        dn2 = igrad[block(b)]
-        scaled = xh2[block(b)]
-        dh1 = dy + norm_back(dn2, g2[...], scaled, rstd2[block(b)])
-        igrad[block(b)] = dh1
+        wfull[tn - 1, b] = facc[wide(b)].astype(BF16)
+        dy = cot[wide(b)].astype(F32)
+        dn2 = igrad[wide(b)]
+        scaled = xh2[wide(b)]
+        dh1 = dy + norm_back(dn2, g2[...], scaled, rstd2[wide(b)])
+        igrad[wide(b)] = dh1
         dob = dh1.astype(BF16)
-        n2s[block(b)] = dob
+        n2s[wide(b)] = dob
         dattn = dot_rt(dob, wout[...])
-        reach = reached(b)
+        lane_id = iota((WR, pw), 1)
+        low_half = lane_id < hw
         for p in range(pairs):
             da = dattn[:, p * pw : (p + 1) * pw]
-            inverse = rsw_s[block(b), p * pw : (p + 1) * pw]
+            inverse = rsw_s[wide(b), p * pw : (p + 1) * pw]
             dnum = da * pltpu.roll(inverse, hw, 1)
-            prod = da * attn[block(b), p * pw : (p + 1) * pw].astype(F32)
+            prod = da * attn[wide(b), p * pw : (p + 1) * pw].astype(F32)
             high = prod.astype(BF16)
             rest = (prod - high.astype(F32)).astype(BF16)
             dden = -dot(jnp.concatenate([high, rest], 1), bsw[...]) * inverse
@@ -829,19 +834,28 @@
             dlo = dden - dhi
             even = jnp.where(lane_id == hw, dhi, jnp.where(lane_id == hw + 1, dlo, 0.0))
             odd = jnp.where(lane_id == 0, dhi, jnp.where(lane_id == 1, dlo, 0.0))
-            even = jnp.where(low_lane, dnum, even)
-            odd = jnp.where(low_lane, odd, dnum)
-            ad[0, block(b), p * pw : (p + 1) * pw] = even.astype(BF16)
-            ad[1, block(b), p * pw : (p + 1) * pw] = odd.astype(BF16)
-            ge = dot_lt(jnp.where(reach, even, 0.0).astype(BF16), phq[p, block(b), :feat_n])
-            go = dot_lt(jnp.where(reach, odd, 0.0).astype(BF16), phq[p, block(b), feat_n:])
-            lst[b, p, :pw] = jnp.where(low_row, ge, go)
-            lst[b, p, pw : pw + 8] = jnp.broadcast_to(ge[hw : hw + 1] + ge[hw + 1 : hw + 2], (8, feat_n))
-            lst[b, p, pw + 8 :] = jnp.broadcast_to(go[0:1] + go[1:2], (8, feat_n))
-
-        @pl.when(b == 1)
+            ad[0, wide(b), p * pw : (p + 1) * pw] = jnp.where(low_half, dnum, even).astype(BF16)
+            ad[1, wide(b), p * pw : (p + 1) * pw] = jnp.where(low_half, odd, dnum).astype(BF16)
+        for c in range(nb // nw):
+            at = b * (nb // nw) + c
+            reach = reached(at)
+            for p in range(pairs):
+                ge, go = (
+                    dot_lt(
+                        jnp.where(reach, ad[o, block(at), p * pw : (p + 1) * pw].astype(F32), 0.0).astype(BF16),
+                        phq[p, block(at), o * feat_n : (o + 1) * feat_n],
+                    )
+                    for o in range(2)
+                )
+                lst[at, p, :pw] = jnp.where(low_row, ge, go)
+                lst[at, p, pw : pw + 8] = jnp.broadcast_to(ge[hw : hw + 1] + ge[hw + 1 : hw + 2], (8, feat_n))
+                lst[at, p, pw + 8 :] = jnp.broadcast_to(go[0:1] + go[1:2], (8, feat_n))
+
+        @pl.when(b == 0)
         def _():
             a_finish(tn - 1)
+            b_finish(3)
+            c_start(3)
 
         return (
             gl2 + jnp.sum(dn2 * scaled, 0, keepdims=True),
@@ -850,8 +864,8 @@
         )
 
     zero_row = jnp.zeros((1, width), F32)
-    gl2, gbo, gbd = lax.fori_loop(0, nb, branch_block, (zero_row,) * 3)
-    store_layer().start()
+    gl2, gbo, gbd = lax.fori_loop(0, nw, branch_block, (zero_row,) * 3)
+    store_layer()
     vec[1:2] = gbo
     vec[2:3] = gl2
     vec[3:4] = gbd
@@ -873,7 +887,7 @@
         return total
 
     def arg_back(darg, x, p):
-        both = dot_rt(darg, featx[p, : 2 * pw])
+        both = dot_rt(darg, featx[p])
         return (both[:, :pw] + (2.0 * x.astype(F32)) * both[:, pw:]) * shrink
 
     out_grad = dot_lt(attn[...], n2s[...])
@@ -905,7 +919,7 @@
         def _():
             k_a_finish(0)
             k_a_finish(1)
-            b_finish(tn - 2)
+            b_finish(2)
 
         @pl.when(i == 3)
         def _():
@@ -914,14 +928,12 @@
         @pl.when(i == 5)
         def _():
             k_a_finish(2)
-            b_finish(tn - 1)
-            c_start(tn - 1)
+            b_finish(0)
 
         @pl.when(i == 7)
         def _():
             k_a_start(3, weight_grad(0, 2, 0, 3))
-            s_b_finish(0)
-            s_b_finish(1)
+            c_start(2)
 
         return 0
 
@@ -973,46 +985,32 @@
         @pl.when(p == 0)
         def _():
             k_a_finish(3)
+            s_b_finish(0)
+            s_b_finish(1)
+
+        @pl.when(p >= 1)
+        def _():
+            k_a_finish(3 + p)
+
+        @pl.when(p == 1)
+        def _():
             s_b_finish(2)
-            for k in range(tn - 2, 0, -2):
-                c_start(k)
-
-        @pl.when(p >= 1)
-        def _():
-            k_a_finish(3 + p)
-
-        @pl.when(p == 1)
-        def _():
+
+        @pl.when(p == 2)
+        def _():
+            c_finish()
+            s_b_finish(3)
             s_middle(0)
             s_middle(1)
-            s_b_finish(3)
-
-        @pl.when(p == 2)
-        def _():
-            c_finish()
+
+        @pl.when(p == 3)
+        def _():
+            s_b_finish(4)
             s_middle(2)
-            s_b_finish(4)
-
-        @pl.when(p == 3)
-        def _():
-            s_c_finish(0)
-            s_c_finish(1)
-            s_middle(3)
-            s_b_finish(5)
 
         return 0
 
     lax.fori_loop(0, pairs, key_pair, 0)
-
-    @pl.when(t < tn - 1)
-    def _():
-        for p in range(pairs):
-            up_copy(p).wait_send()
-
-    @pl.when(t > 0)
-    def _():
-        for p in range(pairs):
-            down_copy(p).wait_send()
 
     def input_block(b, gl1):
         dn1 = dot_rt(wfull[0, b, :WR], wqkv[:, :width])
@@ -1020,52 +1018,51 @@
             dn1 = dn1 + dot_rt(wfull[j, b, :WR], wqkv[:, j * width : (j + 1) * width])
         scaled, inverse = normalized(tok[wide(b)].astype(F32))
         igrad[wide(b)] += norm_back(dn1, g1[...], scaled, inverse)
-        store_grad(b).start()
+        store_grad(b)
 
         @pl.when(b == 0)
         def _():
             k_a_finish(7)
+            s_middle(3)
+
+        @pl.when(b == 1)
+        def _():
+            s_b_finish(5)
             s_middle(4)
-            s_c_finish(2)
-
-        @pl.when(b == 1)
-        def _():
-            k_b_finish(6)
-            d_finish()
 
         return gl1 + jnp.sum(dn1 * scaled, 0, keepdims=True)
 
     vec[0:1] = lax.fori_loop(0, nw, input_block, zero_row)
     va_copy = remote(vec, va, va_s, va_r, core_dev)
     va_copy.start()
-    s_middle(5)
-    s_c_finish(3)
-    va_copy.wait()
+    k_b_finish(6)
+    va_copy.wait_recv()
     vb[0] = vec[...] + va[...]
-    vb_copies = [remote(vb.at[0], vb.at[k], vb_s.at[k - 1], vb_r.at[k - 1], peer_dev(k)) for k in range(1, npeer)]
+    vb_copies = [remote(vb.at[0], vb.at[k], vb_s, vb_r, peer_dev(k)) for k in range(1, npeer)]
     for copy in vb_copies:
         copy.start()
     k_b_finish(7)
-    k_d_finish(0)
-    k_d_finish(1)
-    k_d_finish(2)
+    s_c_finish(0)
+    s_c_finish(1)
+    s_c_finish(2)
+    s_middle(5)
+    s_c_finish(3)
     s_c_finish(4)
-    for copy in vb_copies:
-        copy.wait()
+    arrived(vb.at[pl.ds(1, npeer - 1)], vb_r)
     total = vb[peers[0]]
     for j in range(1, npeer):
         total = total + vb[peers[j]]
     vc[0] = total
-    vc_copies = [remote(vc.at[0], vc.at[k], vc_s.at[k - 1], vc_r.at[k - 1], z_dev(k)) for k in range(1, tn)]
+    vc_copies = [remote(vc.at[0], vc.at[k], vc_s, vc_r, z_dev(k)) for k in range(1, tn)]
     for copy in vc_copies:
         copy.start()
+    k_c_finish(6)
+    k_c_finish(7)
     s_c_finish(5)
-    k_c_finish(6)
-    k_d_finish(3)
-    k_c_finish(7)
-    k_d_finish(4)
-    for copy in vc_copies:
-        copy.wait()
+    d_finish()
+    for i in range(4):
+        k_d_finish(i)
+    arrived(vc.at[pl.ds(1, tn - 1)], vc_r)
     total = vc[zs[0]]
     for j in range(1, tn):
         total = total + vc[zs[j]]
@@ -1074,53 +1071,95 @@
         own = own + vc[k, 4 + k : 5 + k]
     vec_out[...] = total
     vec_out[4:5] = own
+    k_d_finish(4)
+    k_d_finish(6)
+    k_d_finish(7)
     k_d_finish(5)
-    k_d_finish(6)
     e_finish()
-    k_d_finish(7)
-    for i in range(8):
+    store_fin().start()
+    for i in (0, 1, 2, 3, 4, 6, 7, 5):
         k_e_finish(i)
-    store_layer().wait()
-    for b in range(nw):
-        store_grad(b).wait()
+        store_fink(i).start()
+    sent(vec, va_s)
+    sent(vb.at[pl.ds(1, npeer - 1)], vb_s)
+    sent(vc.at[pl.ds(1, tn - 1)], vc_s)
+    sent(gbuf.at[:, 0], a_s)
+    sent(rb, b_s)
+    sent(rc, c_s)
+    sent(fin.at[0, pl.ds(0, (npeer - 1) * rp)], d_s)
+    sent(fin.at[0], e_s)
+    sent(kbuf.at[:, 0], ka_s)
+    sent(krb, kb_s)
+    sent(krc.at[pl.ds(0, 2), pl.ds(1, tn - 1)], kc_s.at[0])
+    sent(krc.at[pl.ds(0, 6), pl.ds(0, levels)], kc_s.at[1])
+    sent(fink.at[:, 0, pl.ds(0, (npeer - 1) * rp)], kd_s)
+    sent(fink.at[:, 0], ke_s)
+
+    @pl.when(t < tn - 1)
+    def _():
+        sent(chf_out, chf_s)
+
+    @pl.when(t > 0)
+    def _():
+        sent(chb_out, chb_s)
+
+    pltpu.make_async_copy(layer_h, layer_h, out_s.at[0]).wait()
+    pltpu.make_async_copy(igrad, igrad_h, out_s.at[1]).wait()
+    store_fin().wait()
+    pltpu.make_async_copy(fink, fink_h, out_s.at[3]).wait()
 
 
 def finish_kernel(
     layer_in, igrad_in, fin_h, fink_h, vec, layer_out, igrad, gwq_h, gwo_h, gwi_h, gwd_h, gl1, gbo, gl2, gbi, gbd,
     layer_v, igrad_v, fin, fink, gwq, gwo, gwi, gwd, in_s, out_s,
 ):
-    def move(i, src, dst, sems):
-        copy = pltpu.make_async_copy(src, dst, sems.at[i])
-        copy.start()
-        return copy
+    used = [0, 0]
+
+    def move(src, dst, out, parts):
+        sems, copies = (in_s, out_s)[out], []
+        size = src.shape[0] // parts
+        for k in range(parts):
+            at = pl.ds(k * size, size)
+            copies.append(pltpu.make_async_copy(src.at[at], dst.at[at], sems.at[used[out]]))
+            used[out] += 1
+            copies[-1].start()
+        return copies
+
+    def wait(copies):
+        for copy in copies:
+            copy.wait()
 
     pairs = fink.shape[0] // 2
     width, pw = fink.shape[2:]
-    kinds = ((fink_h, fink), (fin_h, fin), (layer_in, layer_v), (igrad_in, igrad_v))
-    loads = [move(i, src, dst, in_s) for i, (src, dst) in enumerate(kinds)]
+    a, b, c, d = (
+        move(src, dst, 0, parts)
+        for src, dst, parts in ((fink_h, fink, 8), (fin_h, fin, 2), (layer_in, layer_v, 4), (igrad_in, igrad_v, 4))
+    )
     for row, out in enumerate((gl1, gbo, gl2, gbd, gbi)):
         out[...] = vec[row : row + 1]
-    loads[0].wait()
-    for p in range(pairs):
-        at = slice(p * pw, (p + 1) * pw)
-        gwq[:, at] = fink[2 + p // 2, p % 2].astype(F32)
-        gwq[:, width + p * pw : width + (p + 1) * pw] = fink[4 + p, 0].astype(F32)
-        gwq[:, 2 * width + p * pw : 2 * width + (p + 1) * pw] = fink[4 + p, 1].astype(F32)
-    stores = [move(0, gwq, gwq_h, out_s)]
-    for p in range(pairs):
-        gwo[:, p * pw : (p + 1) * pw] = fink[p // 2, p % 2].astype(F32)
-    stores.append(move(1, gwo, gwo_h, out_s))
-    loads[2].wait()
-    stores.append(move(2, layer_v, layer_out, out_s))
-    loads[3].wait()
-    stores.append(move(3, igrad_v, igrad, out_s))
-    loads[1].wait()
+    wait(a)
+    stores = []
+    quarter = width // 4
+    for k in range(4):
+        rows = pl.ds(k * quarter, quarter)
+        for p in range(pairs):
+            at = slice(p * pw, (p + 1) * pw)
+            gwq[rows, at] = fink[2 + p // 2, p % 2, rows].astype(F32)
+            gwq[rows, width + p * pw : width + (p + 1) * pw] = fink[4 + p, 0, rows].astype(F32)
+            gwq[rows, 2 * width + p * pw : 2 * width + (p + 1) * pw] = fink[4 + p, 1, rows].astype(F32)
+            gwo[rows, at] = fink[p // 2, p % 2, rows].astype(F32)
+        stores += move(gwq.at[rows], gwq_h.at[rows], 1, 1)
+        stores += move(gwo.at[rows], gwo_h.at[rows], 1, 1)
+    wait(b)
     gwi[...] = fin[0].astype(F32)
-    stores.append(move(4, gwi, gwi_h, out_s))
+    stores += move(gwi, gwi_h, 1, 2)
+    wait(c)
+    stores += move(layer_v, layer_out, 1, 2)
+    wait(d)
+    stores += move(igrad_v, igrad, 1, 4)
     gwd[...] = fin[1].astype(F32).T
-    stores.append(move(5, gwd, gwd_h, out_s))
-    for copy in stores:
-        copy.wait()
+    stores += move(gwd, gwd_h, 1, 2)
+    wait(stores)
 
 
 def local(
@@ -1164,15 +1203,19 @@
             jax.ShapeDtypeStruct((vrows, width), F32),
         ),
         in_specs=[pl.BlockSpec(memory_space=pltpu.SMEM)]
-        + [anywhere, anywhere, anywhere, vmem, anywhere, anywhere, vmem, vmem, anywhere, anywhere],
-        out_specs=(anywhere, anywhere, vmem, vmem, vmem),
+        + [anywhere] * 10,
+        out_specs=(anywhere,) * 4 + (vmem,),
         scratch_shapes=[
+            scratch((2, width, width)),
+            scratch((8, 2, width, pw)),
+            scratch((1, width), F32),
+            scratch((1, width), F32),
+            scratch((1, 2 * width + ffl), F32),
             scratch((rows_n, width)),
             scratch((rows_n, width)),
             scratch((heads, hw, feat_n)),
             scratch((width, 3 * width)),
             scratch((width, width)),
-            scratch((rows_n, width)),
             scratch((rows_n, width), F32),
             scratch((tn, 2, width, ffl)),
             scratch((tn, 8, ffl), F32),
@@ -1182,7 +1225,8 @@
             scratch((pairs, rows_n, pw)),
             scratch((pairs, rows_n, 2 * feat_n)),
             scratch((pairs, rows_n, 2 * feat_n)),
-            scratch((pairs, 3 * pw, 2 * feat_n)),
+            scratch((pairs, 2 * pw, 2 * feat_n)),
+            scratch((2 * pw, 2 * pw)),
             scratch((2 * pw, pw)),
             scratch((nb, BR, BR)),
             scratch((nb, BR, BR)),
@@ -1211,46 +1255,46 @@
             scratch((vrows, width), F32),
             scratch((npeer, vrows, width), F32),
             scratch((tn, vrows, width), F32),
-            dma((7,)),
-            dma((1 + rows_n // WR,)),
+            dma((10,)),
+            dma((4,)),
+            dma(()),
+            dma(()),
+            dma(()),
             dma((tn - 1,)),
+            dma(()),
             dma((tn - 1,)),
+            dma(()),
             dma((tn - 1,)),
+            dma(()),
+            dma((pairs,)),
+            dma(()),
+            dma((pairs,)),
+            dma(()),
+            dma((2,)),
+            dma(()),
+            dma((tn,)),
+            dma(()),
             dma((tn - 1,)),
-            dma((tn - 1, npeer - 1)),
-            dma((tn - 1, npeer - 1)),
-            dma((tn - 1,)),
-            dma((tn - 1,)),
-            dma((pairs,)),
-            dma((pairs,)),
-            dma((pairs,)),
-            dma((pairs,)),
-            dma((tn,)),
-            dma((tn,)),
-            dma((tn, npeer - 1)),
-            dma((tn, npeer - 1)),
-            dma((tn - 1,)),
-            dma((tn - 1,)),
-            dma((npeer - 1,)),
-            dma((npeer - 1,)),
-            dma(()),
+            dma(()),
+            dma(()),
+            dma(()),
+            dma(()),
+            dma(()),
+            dma((4,)),
             dma(()),
             dma((8,)),
+            dma((2,)),
+            dma((8, (tn - 1).bit_length())),
+            dma(()),
             dma((8,)),
-            dma((8, npeer - 1)),
-            dma((8, npeer - 1)),
-            dma((8, tn - 1)),
-            dma((8, tn - 1)),
-            dma((8, npeer - 1)),
-            dma((8, npeer - 1)),
+            dma(()),
             dma((8,)),
-            dma((8,)),
-            dma(()),
-            dma(()),
-            dma((npeer - 1,)),
-            dma((npeer - 1,)),
-            dma((tn - 1,)),
-            dma((tn - 1,)),
+            dma(()),
+            dma(()),
+            dma(()),
+            dma(()),
+            dma(()),
+            dma(()),
         ],
         compiler_params=pltpu.CompilerParams(
             collective_id=0, has_side_effects=True, vmem_limit_bytes=63 * 1024 * 1024
@@ -1263,7 +1307,7 @@
         ln1_gain[None],
         w_qkv,
         w_out,
-        jnp.stack([b_out, b_in, b_down]).astype(F32),
+        lax.optimization_barrier(jnp.concatenate([b_out, b_in, b_down]).astype(F32))[None],
         ln2_gain[None],
         w_in,
         w_down,
@@ -1287,8 +1331,8 @@
             scratch((width, width), F32),
             scratch((width, width), F32),
             scratch((width, width), F32),
-            dma((4,)),
-            dma((6,)),
+            dma((18,)),
+            dma((18,)),
         ],
         compiler_params=pltpu.CompilerParams(vmem_limit_bytes=63 * 1024 * 1024),
     )(*out)

time: 127 us -> 113 us (0.89)
  Pallas kernels: 123 us -> 111 us
  local copies, waits for them, and re-layouts: 2.05 us -> 0.6 us
    pallas_call x1, Pallas kernels: 116 us -> 104 us  [local(): pl.pallas_call(functools.partial(layer_kernel, tn, dpn), out_shape=(jax.S...]
    another operation x3 -> x0, local copies, waits for them, and re-layouts: 2.05 us -> none  [local(): jnp.stack([b_out, b_in, b_down]).astype(F32)]
where the time goes in v3:
time: 113 us
  Pallas kernels  111 us (98%)
    pallas_call x1, Pallas kernels, local(): pl.pallas_call(functools.partial(layer_kernel, tn, dpn), out_shape=(jax.S...  104 us
    pallas_call x1, Pallas kernels, local(): pl.pallas_call(finish_kernel, out_shape=(out[0], out[1], square(3), squar...  6.82 us

profile of v3, /device:TPU:0, one launch (start us, length us, event | category | flops | bytes accessed | tf_op | source)
XLA Modules:
  0.0 113.2 jit_solution(12748412874812041371)
XLA Ops:
  0.6 0.7 maximum_convert_fusion
  1.4 0.6 broadcast_in_dim.10.biases_h
  2.0 104.2 %shard_map.212 = (bf16[1024,512]{1,0:T(8,128)(2,1)}, f32[1024,512]{1,0:T(8,128)}, bf16[2,512,512]{2,1,0:T(8,128)(2,1)}, bf16[8,2,512,128]{3,2,1,0:T(8,128)(2,1)}, f32[8,512]{1,0:T(8,128)}) custom-call(s32[1,2]{1,0:T(1,128)} %lens.1, bf16[1024,512]{1,0:T(8,128)(2,1)} %tok_h.1, bf16[1024,512]{1,0:T(8,128)(2,1)} %cot_h.1, bf16[8,64,256]{2,1,0:T(8,128)(2,1)} %feats_h.1, ...), custom_call_target="tpu_custom_call" | custom-call | tf_op jit(solution)/shard_map/pallas_call | solution.py:1196
  106.2 6.8 %shard_map.213 = (bf16[1024,512]{1,0:T(8,128)(2,1)}, f32[1024,512]{1,0:T(8,128)}, f32[512,1536]{1,0:T(8,128)}, f32[512,512]{1,0:T(8,128)}, f32[512,512]{1,0:T(8,...) custom-call(bf16[1024,512]{1,0:T(8,128)(2,1)} %get-tuple-element.27., ...), custom_call_target="tpu_custom_call" | custom-call | tf_op jit(solution)/shard_map/pallas_call | solution.py:1320

commit v4 on v3

--- a/solution.py
+++ b/solution.py
@@ -51,10 +51,12 @@
     g1_h,
     wqkv_h,
     wout_h,
-    biases_h,
+    bout_h,
     g2_h,
     win_h,
+    bin_h,
     wdn_h,
+    bdn_h,
     layer_h,
     igrad_h,
     fin_h,
@@ -64,7 +66,9 @@
     fink,
     g1,
     g2,
-    biases,
+    bout,
+    bin_,
+    bdn,
     tok,
     cot,
     feats,
@@ -191,7 +195,9 @@
         "feats": (feats_h, feats),
         "g1": (g1_h, g1),
         "g2": (g2_h, g2),
-        "biases": (biases_h, biases),
+        "bout": (bout_h, bout),
+        "bin": (bin_h, bin_),
+        "bdn": (bdn_h, bdn),
         "win": (win_h, wfull.at[0, 0]),
         "wdn": (wdn_h, wfull.at[0, 1]),
         "tok": (tok_h, tok),
@@ -531,11 +537,14 @@
     def lanes(p):
         return pl.ds(pl.multiple_of(p * pw, pw), pw)
 
+    def as_row(ref):
+        return ref[...].astype(F32).reshape(1, ref.shape[0])
+
     low_lane = iota((BR, pw), 1) < hw
     low_row = iota((pw, feat_n), 0) < hw
     row_id = iota((pw, feat_n), 0)
 
-    for name in ("feats", "g1", "g2", "biases"):
+    for name in ("feats", "g1", "g2", "bout", "bin", "bdn"):
         loads[name].wait()
     featx[...] = jnp.zeros_like(featx)
     for p in range(pairs):
@@ -574,7 +583,7 @@
     loads["win"].wait()
     loads["wdn"].wait()
     pl.semaphore_wait(bar, len(targets))
-    bfull[0] = jnp.broadcast_to(biases[:, width : width + bfull.shape[2]], bfull.shape[1:])
+    bfull[0] = jnp.broadcast_to(as_row(bin_), bfull.shape[1:])
     for k in range(1, tn):
         bz_copy(k).start()
     wz_copy(1).start()
@@ -720,12 +729,12 @@
     lax.fori_loop(0, pairs, attend_pair, 0)
 
     def hidden_block(b, _):
-        h1 = tok[wide(b)].astype(F32) + (dot(attn[wide(b)], wout[...]) + biases[:, :width])
+        h1 = tok[wide(b)].astype(F32) + (dot(attn[wide(b)], wout[...]) + as_row(bout))
         scaled, inverse = normalized(h1)
         xh2[wide(b)] = scaled
         rstd2[wide(b)] = inverse
         n2s[wide(b)] = (scaled * g2[...]).astype(BF16)
-        facc[wide(b)] = h1 + biases[:, width + bfull.shape[2] :]
+        facc[wide(b)] = h1 + as_row(bdn)
         return 0
 
     loads["wout"].wait()
@@ -1203,14 +1212,16 @@
             jax.ShapeDtypeStruct((vrows, width), F32),
         ),
         in_specs=[pl.BlockSpec(memory_space=pltpu.SMEM)]
-        + [anywhere] * 10,
+        + [anywhere] * 12,
         out_specs=(anywhere,) * 4 + (vmem,),
         scratch_shapes=[
             scratch((2, width, width)),
             scratch((8, 2, width, pw)),
             scratch((1, width), F32),
             scratch((1, width), F32),
-            scratch((1, 2 * width + ffl), F32),
+            scratch((width,)),
+            scratch((ffl,)),
+            scratch((width,)),
             scratch((rows_n, width)),
             scratch((rows_n, width)),
             scratch((heads, hw, feat_n)),
@@ -1255,7 +1266,7 @@
             scratch((vrows, width), F32),
             scratch((npeer, vrows, width), F32),
             scratch((tn, vrows, width), F32),
-            dma((10,)),
+            dma((12,)),
             dma((4,)),
             dma(()),
             dma(()),
@@ -1307,10 +1318,12 @@
         ln1_gain[None],
         w_qkv,
         w_out,
-        lax.optimization_barrier(jnp.concatenate([b_out, b_in, b_down]).astype(F32))[None],
+        b_out,
         ln2_gain[None],
         w_in,
+        b_in,
         w_down,
+        b_down,
     )
     row = jax.ShapeDtypeStruct((1, width), F32)
 

time: 113 us -> 112 us (level)
  no operation moved by 1% of the time
where the time goes in v4:
time: 112 us; the launch traced here: 111 us
  Pallas kernels  111 us (99%)
    pallas_call x1, Pallas kernels, local(): pl.pallas_call(functools.partial(layer_kernel, tn, dpn), out_shape=(jax.S...  104 us
    pallas_call x1, Pallas kernels, local(): pl.pallas_call(finish_kernel, out_shape=(out[0], out[1], square(3), squar...  6.82 us

profile of v4, /device:TPU:0, one launch (start us, length us, event | category | flops | bytes accessed | tf_op | source)
XLA Modules:
  0.0 111.4 jit_solution(4182555927745397366)
XLA Ops:
  0.6 103.7 %shard_map.212 = (bf16[1024,512]{1,0:T(8,128)(2,1)}, f32[1024,512]{1,0:T(8,128)}, bf16[2,512,512]{2,1,0:T(8,128)(2,1)}, bf16[8,2,512,128]{3,2,1,0:T(8,128)(2,1)}, f32[8,512]{1,0:T(8,128)}) custom-call(s32[1,2]{1,0:T(1,128)} %lens.1, bf16[1024,512]{1,0:T(8,128)(2,1)} %tok_h.1, bf16[1024,512]{1,0:T(8,128)(2,1)} %cot_h.1, bf16[8,64,256]{2,1,0:T(8,128)(2,1)} %feats_h.1, ...), custom_call_target="tpu_custom_call" | custom-call | tf_op jit(solution)/shard_map/pallas_call | solution.py:1205
  104.4 6.8 %shard_map.213 = (bf16[1024,512]{1,0:T(8,128)(2,1)}, f32[1024,512]{1,0:T(8,128)}, f32[512,1536]{1,0:T(8,128)}, f32[512,512]{1,0:T(8,128)}, f32[512,512]{1,0:T(8,...) custom-call(bf16[1024,512]{1,0:T(8,128)(2,1)} %get-tuple-element.27., ...), custom_call_target="tpu_custom_call" | custom-call | tf_op jit(solution)/shard_map/pallas_call | solution.py:1333

commit v5 on v4

--- a/solution.py
+++ b/solution.py
@@ -61,6 +61,7 @@
     igrad_h,
     fin_h,
     fink_h,
+    vec_h,
     vec_out,
     fin,
     fink,
@@ -1080,6 +1081,7 @@
         own = own + vc[k, 4 + k : 5 + k]
     vec_out[...] = total
     vec_out[4:5] = own
+    pltpu.make_async_copy(vec_out, vec_h, out_s.at[4]).start()
     k_d_finish(4)
     k_d_finish(6)
     k_d_finish(7)
@@ -1112,6 +1114,7 @@
     def _():
         sent(chb_out, chb_s)
 
+    pltpu.make_async_copy(vec_out, vec_h, out_s.at[4]).wait()
     pltpu.make_async_copy(layer_h, layer_h, out_s.at[0]).wait()
     pltpu.make_async_copy(igrad, igrad_h, out_s.at[1]).wait()
     store_fin().wait()
@@ -1119,56 +1122,46 @@
 
 
 def finish_kernel(
-    layer_in, igrad_in, fin_h, fink_h, vec, layer_out, igrad, gwq_h, gwo_h, gwi_h, gwd_h, gl1, gbo, gl2, gbi, gbd,
-    layer_v, igrad_v, fin, fink, gwq, gwo, gwi, gwd, in_s, out_s,
+    layer_in, igrad_in, fin_h, fink_h, vec_h, layer_out, igrad, gwq_h, gwo_h, gwi_h, gwd_h, gl1, gbo, gl2, gbi, gbd,
+    layer_v, igrad_v, fin, fink, vec, rows_v, gwq, gwo, gwi, gwd, in_s, out_s,
 ):
-    used = [0, 0]
-
-    def move(src, dst, out, parts):
-        sems, copies = (in_s, out_s)[out], []
-        size = src.shape[0] // parts
-        for k in range(parts):
-            at = pl.ds(k * size, size)
-            copies.append(pltpu.make_async_copy(src.at[at], dst.at[at], sems.at[used[out]]))
-            used[out] += 1
-            copies[-1].start()
-        return copies
-
-    def wait(copies):
-        for copy in copies:
-            copy.wait()
+    def move(src, dst, sem):
+        copy = pltpu.make_async_copy(src, dst, sem)
+        copy.start()
+        return copy
 
     pairs = fink.shape[0] // 2
     width, pw = fink.shape[2:]
-    a, b, c, d = (
-        move(src, dst, 0, parts)
-        for src, dst, parts in ((fink_h, fink, 8), (fin_h, fin, 2), (layer_in, layer_v, 4), (igrad_in, igrad_v, 4))
-    )
-    for row, out in enumerate((gl1, gbo, gl2, gbd, gbi)):
-        out[...] = vec[row : row + 1]
-    wait(a)
+    kinds = ((fink_h, fink), (layer_in, layer_v), (igrad_in, igrad_v), (fin_h, fin), (vec_h, vec))
+    a, b, c, d, e = (move(src, dst, in_s.at[n]) for n, (src, dst) in enumerate(kinds))
     stores = []
-    quarter = width // 4
-    for k in range(4):
-        rows = pl.ds(k * quarter, quarter)
+    a.wait()
+    for k in range(2):
+        rows = pl.ds(k * width // 2, width // 2)
         for p in range(pairs):
             at = slice(p * pw, (p + 1) * pw)
             gwq[rows, at] = fink[2 + p // 2, p % 2, rows].astype(F32)
             gwq[rows, width + p * pw : width + (p + 1) * pw] = fink[4 + p, 0, rows].astype(F32)
             gwq[rows, 2 * width + p * pw : 2 * width + (p + 1) * pw] = fink[4 + p, 1, rows].astype(F32)
-            gwo[rows, at] = fink[p // 2, p % 2, rows].astype(F32)
-        stores += move(gwq.at[rows], gwq_h.at[rows], 1, 1)
-        stores += move(gwo.at[rows], gwo_h.at[rows], 1, 1)
-    wait(b)
+        stores.append(move(gwq.at[rows], gwq_h.at[rows], out_s.at[k]))
+    b.wait()
+    stores.append(move(layer_v, layer_out, out_s.at[2]))
+    c.wait()
+    stores.append(move(igrad_v, igrad, out_s.at[3]))
+    for p in range(pairs):
+        gwo[:, p * pw : (p + 1) * pw] = fink[p // 2, p % 2].astype(F32)
+    stores.append(move(gwo, gwo_h, out_s.at[4]))
+    d.wait()
     gwi[...] = fin[0].astype(F32)
-    stores += move(gwi, gwi_h, 1, 2)
-    wait(c)
-    stores += move(layer_v, layer_out, 1, 2)
-    wait(d)
-    stores += move(igrad_v, igrad, 1, 4)
+    stores.append(move(gwi, gwi_h, out_s.at[5]))
     gwd[...] = fin[1].astype(F32).T
-    stores += move(gwd, gwd_h, 1, 2)
-    wait(stores)
+    stores.append(move(gwd, gwd_h, out_s.at[6]))
+    e.wait()
+    for row, out in enumerate((gl1, gbo, gl2, gbd, gbi)):
+        rows_v[row] = vec[row : row + 1]
+        stores.append(move(rows_v.at[row], out, out_s.at[7 + row]))
+    for copy in stores:
+        copy.wait()
 
 
 def local(
@@ -1196,7 +1189,6 @@
     rp = width // npeer
     vrows = -(-(4 + tn) // 8) * 8
     dma = pltpu.SemaphoreType.DMA
-    vmem = pl.BlockSpec(memory_space=pltpu.VMEM)
     anywhere = pl.BlockSpec(memory_space=pl.ANY)
 
     def scratch(shape, dtype=BF16):
@@ -1213,8 +1205,9 @@
         ),
         in_specs=[pl.BlockSpec(memory_space=pltpu.SMEM)]
         + [anywhere] * 12,
-        out_specs=(anywhere,) * 4 + (vmem,),
+        out_specs=(anywhere,) * 5,
         scratch_shapes=[
+            scratch((vrows, width), F32),
             scratch((2, width, width)),
             scratch((8, 2, width, pw)),
             scratch((1, width), F32),
@@ -1267,7 +1260,7 @@
             scratch((npeer, vrows, width), F32),
             scratch((tn, vrows, width), F32),
             dma((12,)),
-            dma((4,)),
+            dma((5,)),
             dma(()),
             dma(()),
             dma(()),
@@ -1333,19 +1326,21 @@
     done = pl.pallas_call(
         finish_kernel,
         out_shape=(out[0], out[1], square(3), square(1), square(1), square(1)) + (row,) * 5,
-        in_specs=[anywhere] * 4 + [vmem],
-        out_specs=(anywhere,) * 6 + (vmem,) * 5,
+        in_specs=[anywhere] * 5,
+        out_specs=(anywhere,) * 11,
         scratch_shapes=[
             scratch((rows_n, width)),
             scratch((rows_n, width), F32),
             scratch((2, width, width)),
             scratch((8, 2, width, pw)),
+            scratch((vrows, width), F32),
+            scratch((5, 1, width), F32),
             scratch((width, 3 * width), F32),
             scratch((width, width), F32),
             scratch((width, width), F32),
             scratch((width, width), F32),
-            dma((18,)),
-            dma((18,)),
+            dma((5,)),
+            dma((12,)),
         ],
         compiler_params=pltpu.CompilerParams(vmem_limit_bytes=63 * 1024 * 1024),
     )(*out)

time: 112 us -> 110 us (0.982)
  Pallas kernels: 111 us -> 109 us
    pallas_call x1, Pallas kernels: 6.82 us -> 5.57 us  [local(): pl.pallas_call(finish_kernel, out_shape=(out[0], out[1], square(3), squar...]
where the time goes in v5:
time: 110 us
  Pallas kernels  109 us (99%)
    pallas_call x1, Pallas kernels, local(): pl.pallas_call(functools.partial(layer_kernel, tn, dpn), out_shape=(jax.S...  103 us
    pallas_call x1, Pallas kernels, local(): pl.pallas_call(finish_kernel, out_shape=(out[0], out[1], square(3), squar...  5.57 us

profile of v5, /device:TPU:0, one launch (start us, length us, event | category | flops | bytes accessed | tf_op | source)
XLA Modules:
  0.0 109.5 jit_solution(5875948321633949935)
XLA Ops:
  0.6 103.1 %shard_map.212 = (bf16[1024,512]{1,0:T(8,128)(2,1)}, f32[1024,512]{1,0:T(8,128)}, bf16[2,512,512]{2,1,0:T(8,128)(2,1)}, bf16[8,2,512,128]{3,2,1,0:T(8,128)(2,1)}, f32[8,512]{1,0:T(8,128)}) custom-call(s32[1,2]{1,0:T(1,128)} %lens.1, bf16[1024,512]{1,0:T(8,128)(2,1)} %tok_h.1, bf16[1024,512]{1,0:T(8,128)(2,1)} %cot_h.1, bf16[8,64,256]{2,1,0:T(8,128)(2,1)} %feats_h.1, ...), custom_call_target="tpu_custom_call" | custom-call | tf_op jit(solution)/shard_map/pallas_call | solution.py:1197
  103.8 5.6 %shard_map.213 = (bf16[1024,512]{1,0:T(8,128)(2,1)}, f32[1024,512]{1,0:T(8,128)}, f32[512,1536]{1,0:T(8,128)}, f32[512,512]{1,0:T(8,128)}, f32[512,512]{1,0:T(8,...) custom-call(bf16[1024,512]{1,0:T(8,128)(2,1)} %get-tuple-element.27., ...), custom_call_target="tpu_custom_call" | custom-call | tf_op jit(solution)/shard_map/pallas_call | solution.py:1326

commit v6 on v5

--- a/solution.py
+++ b/solution.py
@@ -199,10 +199,10 @@
         "bout": (bout_h, bout),
         "bin": (bin_h, bin_),
         "bdn": (bdn_h, bdn),
+        "tok": (tok_h, tok),
+        "wqkv": (wqkv_h, wqkv),
         "win": (win_h, wfull.at[0, 0]),
         "wdn": (wdn_h, wfull.at[0, 1]),
-        "tok": (tok_h, tok),
-        "wqkv": (wqkv_h, wqkv),
         "wout": (wout_h, wout),
         "cot": (cot_h, cot),
     }
@@ -554,11 +554,8 @@
             featx[p, pw + o * hw : pw + (o + 1) * hw, o * feat_n : (o + 1) * feat_n] = jnp.full(
                 (hw, feat_n), -0.5, BF16
             )
-    ri, ci = iota((2 * pw, pw), 0), iota((2 * pw, pw), 1)
     ro, co = iota((2 * pw, 2 * pw), 0), iota((2 * pw, 2 * pw), 1)
     norms[...] = jnp.where((lax.rem(ro, pw) < hw) == (co < pw), -0.5, 0.0).astype(BF16)
-    swap = (lax.rem(ri, pw) < hw) != (ci < hw)
-    bsw[...] = jnp.where(swap, 1.0, 0.0).astype(BF16)
 
     def build_mask(b, _):
         seg_i = seg_array((BR, BR), 0, first + b * BR)
@@ -566,7 +563,6 @@
         same = seg_i == seg_j
         i, j = iota((BR, BR), 0), iota((BR, BR), 1)
         mask[b] = jnp.where(same & (i >= j), 1.0, 0.0).astype(BF16)
-        maskt[b] = jnp.where(same & (j >= i), 1.0, 0.0).astype(BF16)
         return 0
 
     lax.fori_loop(0, nb, build_mask, 0)
@@ -577,18 +573,15 @@
     def _():
         chf_in[...] = jnp.zeros_like(chf_in)
 
-    @pl.when(t == tn - 1)
-    def _():
-        chb_in[...] = jnp.zeros_like(chb_in)
 
     loads["win"].wait()
     loads["wdn"].wait()
     pl.semaphore_wait(bar, len(targets))
     bfull[0] = jnp.broadcast_to(as_row(bin_), bfull.shape[1:])
+    wz_copy(1).start()
+    wz_copy(2).start()
     for k in range(1, tn):
         bz_copy(k).start()
-    wz_copy(1).start()
-    wz_copy(2).start()
 
     def features_of(x, p):
         wide = x.astype(F32)
@@ -699,6 +692,23 @@
         return 0
 
     lax.fori_loop(0, pairs, inside_pair, 0)
+
+    ri, ci = iota((2 * pw, pw), 0), iota((2 * pw, pw), 1)
+    swap = (lax.rem(ri, pw) < hw) != (ci < hw)
+    bsw[...] = jnp.where(swap, 1.0, 0.0).astype(BF16)
+
+    def build_turned(b, _):
+        seg_i = seg_array((BR, BR), 0, first + b * BR)
+        seg_j = seg_array((BR, BR), 1, first + b * BR)
+        later = iota((BR, BR), 1) >= iota((BR, BR), 0)
+        maskt[b] = jnp.where((seg_i == seg_j) & later, 1.0, 0.0).astype(BF16)
+        return 0
+
+    lax.fori_loop(0, nb, build_turned, 0)
+
+    @pl.when(t == tn - 1)
+    def _():
+        chb_in[...] = jnp.zeros_like(chb_in)
 
     def attend_pair(p, _):
         up_slots(slot + pairs + p, slot + pairs, slot + 2 * pairs)
@@ -782,13 +792,13 @@
             def _():
                 a_finish(jnp.maximum(turn - 1, 0))
 
-            @pl.when((turn == 0) & (b == 0))
-            def _():
-                w_swap(2)
-
             @pl.when((turn == 0) & (b == nw - 1))
             def _():
                 w_swap(3)
+
+            @pl.when((turn == 1) & (b == 0))
+            def _():
+                w_swap(2)
 
             return total + jnp.sum(du.astype(F32), 0, keepdims=True)
 

time: 110 us -> 110 us (level)
  no operation moved by 1% of the time
where the time goes in v6:
time: 110 us; the launch traced here: 109 us
  Pallas kernels  109 us (99%)
    pallas_call x1, Pallas kernels, local(): pl.pallas_call(functools.partial(layer_kernel, tn, dpn), out_shape=(jax.S...  103 us
    pallas_call x1, Pallas kernels, local(): pl.pallas_call(finish_kernel, out_shape=(out[0], out[1], square(3), squar...  5.57 us

profile of v6, /device:TPU:0, one launch (start us, length us, event | category | flops | bytes accessed | tf_op | source)
XLA Modules:
  0.0 109.4 jit_solution(13587424024744112583)
XLA Ops:
  0.6 103.0 %shard_map.212 = (bf16[1024,512]{1,0:T(8,128)(2,1)}, f32[1024,512]{1,0:T(8,128)}, bf16[2,512,512]{2,1,0:T(8,128)(2,1)}, bf16[8,2,512,128]{3,2,1,0:T(8,128)(2,1)}, f32[8,512]{1,0:T(8,128)}) custom-call(s32[1,2]{1,0:T(1,128)} %lens.1, bf16[1024,512]{1,0:T(8,128)(2,1)} %tok_h.1, bf16[1024,512]{1,0:T(8,128)(2,1)} %cot_h.1, bf16[8,64,256]{2,1,0:T(8,128)(2,1)} %feats_h.1, ...), custom_call_target="tpu_custom_call" | custom-call | tf_op jit(solution)/shard_map/pallas_call | solution.py:1207
  103.7 5.6 %shard_map.213 = (bf16[1024,512]{1,0:T(8,128)(2,1)}, f32[1024,512]{1,0:T(8,128)}, f32[512,1536]{1,0:T(8,128)}, f32[512,512]{1,0:T(8,128)}, f32[512,512]{1,0:T(8,...) custom-call(bf16[1024,512]{1,0:T(8,128)(2,1)} %get-tuple-element.27., ...), custom_call_target="tpu_custom_call" | custom-call | tf_op jit(solution)/shard_map/pallas_call | solution.py:1336
